TPU v7x, 512 devices: a whole 4x8x8 slice. The times are simulated.
512 devices in a mesh: leaf: 128 (over x, y_hi, z, core), col: 4 (over y_lo).
Axes of the slice: x: 4, y: 8 (y_hi: 2, y_lo: 4; y = y_hi * 4 + y_lo), z: 8, core: 2. Of those that a mesh axis runs over, the one named last changes fastest.
Arguments:
- leaf_inverse: float32 [256, 1024, 1024], P('leaf', 'col'), may hold values from -1 to 3, as said below
- left_gen: float32 [256, 1024, 256], P('leaf', 'col'), may hold values from -0.125 to 0.125
- right_gen: float32 [256, 1024, 256], P('leaf', 'col'), may hold values from -0.125 to 0.125
- parent_gen: float32 [256, 1024, 256], P('leaf', 'col'), may hold values from -6 to 6
Outputs:
- updated_gen: float32 [256, 1024, 256], P('leaf', 'col')
Inputs may be any that keep to these rules, and one draw needn't show every extreme that they name: `leaf_inverse`: the inverse of a leaf block of the kernel matrix, of full rank.
All inputs are finite; a program needn't handle non-finite values.
Results may differ from a plain program's by a relative error of at most 0.000076.
Values sent between devices are 32-bit elements; how exact they have to be, the bound alone decides.
No kernel may reach another device: no remote copies, remote signals or barrier semaphores. Data moves between devices by JAX's collectives and lax.ppermute only.
A program may use at most 64 MiB of HBM per device.

v0:
```python
import jax
import jax.numpy as jnp
from jax import lax
from jax.sharding import PartitionSpec as P

LEVEL = 2


precise = lax.Precision.HIGHEST


def partner(shard, axis, distance):
    return lax.ppermute(shard, axis, [(i, i ^ 1 << distance) for i in range(lax.axis_size(axis))])


def invert_block(square):
    width = square.shape[-1]
    places = jnp.arange(width, dtype=jnp.int32)
    identity_b = jnp.broadcast_to(jnp.eye(width, dtype=jnp.float32), square.shape)
    joined = jnp.concatenate((square, identity_b), axis=2)

    def eliminate(step, current):
        pivot_row = lax.dynamic_slice_in_dim(current, step, 1, 1)[:, 0, :]
        pivot = lax.dynamic_slice_in_dim(pivot_row, step, 1, 1)
        pivot_row = pivot_row / pivot
        selector = (places == step).astype(jnp.float32)
        column = jnp.sum(current[:, :, :width] * selector[None, None, :], axis=2)
        current = current - column[:, :, None] * pivot_row[:, None, :]
        return current + selector[None, :, None] * pivot_row[:, None, :]

    joined = lax.fori_loop(0, width, eliminate, joined)
    return joined[:, :, width:]


def block_solve(matrix, target):
    order_k = matrix.shape[-1]
    block = 32
    joined = jnp.concatenate((matrix, target), axis=2)
    for start in range(0, order_k, block):
        finish = start + block
        pivot_inverse = invert_block(joined[:, start:finish, start:finish])
        row_band = jnp.einsum(
            "lab,lbc->lac", pivot_inverse, joined[:, start:finish, :], precision=precise
        )
        column_band = joined[:, :, start:finish]
        updated = joined - jnp.einsum("lab,lbc->lac", column_band, row_band, precision=precise)
        joined = updated.at[:, start:finish, :].set(row_band)
    return joined[:, :, order_k:]


def solve_reduced(sibling_g, own_g, target):
    order_k = own_g.shape[-1]
    reduced = jnp.eye(order_k, dtype=jnp.float32) - jnp.einsum(
        "lab,lbc->lac", sibling_g, own_g, precision=precise
    )
    return block_solve(reduced, target)


def body(leaf_inverse, left_gen, right_gen, parent_gen):
    leaves_here, rows_here, order_k = left_gen.shape
    first = jnp.einsum(
        "lrm,lmk->lrk",
        leaf_inverse,
        lax.all_gather(left_gen, "col", axis=1, tiled=True),
        precision=precise,
    )
    second = jnp.einsum(
        "lrm,lmk->lrk",
        leaf_inverse,
        lax.all_gather(parent_gen, "col", axis=1, tiled=True),
        precision=precise,
    )
    partial_g = jnp.einsum("lrk,lrj->lkj", right_gen, first, precision=precise)
    partial_h = jnp.einsum("lrk,lrj->lkj", right_gen, second, precision=precise)
    own_g, own_h = lax.psum((partial_g, partial_h), "col")
    joined = jnp.concatenate((own_g, own_h), axis=2)
    arrived = partner(joined, "leaf", LEVEL)
    sibling_g = arrived[:, :, :order_k]
    sibling_h = arrived[:, :, order_k:]
    target = sibling_h - jnp.einsum("lab,lbc->lac", sibling_g, own_h, precision=precise)
    coeffs = solve_reduced(sibling_g, own_g, target)
    return second - jnp.einsum("lrk,lkj->lrj", first, coeffs, precision=precise)


def solution(mesh):
    return jax.shard_map(
        body,
        mesh=mesh,
        in_specs=(
            P("leaf", "col", None),
            P("leaf", "col", None),
            P("leaf", "col", None),
            P("leaf", "col", None),
        ),
        out_specs=P("leaf", "col", None),
        check_vma=False,
    )
```

profile of v0, /device:TPU:6, one launch (start us, length us, event | category | flops | bytes accessed | tf_op | source)
XLA Modules:
  0.0 494.1 jit_solution(5693871024862172785)
XLA Ops:
  8.1 59.0 %all-gather.3.cloned.1.call-done = f32[2,1024,256]{2,1,0:T(8,128)} async-done(((f32[2,256,256]{2,1,0:T(8,128)}), f32[2,1024,256]{2,1,0:T(8,128)}) %all-gather.3.cloned.1.call-update) | async-done | bytes 2097168 | tf_op jit(solution)/shard_map/all_gather | solution.py:70
  67.0 3.7 fusion.62
  72.5 49.2 %all-gather.5.cloned.1.call-done = f32[2,1024,256]{2,1,0:T(8,128)} async-done(((f32[2,256,256]{2,1,0:T(8,128)}), f32[2,1024,256]{2,1,0:T(8,128)}) %all-gather.5.cloned.1.call-update) | async-done | bytes 2097168 | tf_op jit(solution)/shard_map/all_gather | solution.py:64
  121.8 3.7 fusion.63
  127.4 69.5 %all-reduce.3.cloned.1.call-done = (f32[2,256,256]{1,2,0:T(8,128)}, f32[2,256,256]{1,2,0:T(8,128)}) async-done(((f32[2,256,256]{1,2,0:T(8,128)}, f32[2,256,256]{1,2,0:T(8,128)}), (f32[2,256,256]{1,2,0:T(8,128)}, f32[2,256,256]{1,2,0:T(8,128)})) %all-reduce.3.cloned.1.call-update) | async-done | bytes 1048592 | tf_op jit(solution)/shard_map/psum | solution.py:75
  199.2 4.8 collective-permute-start
  204.1 45.5 %collective-permute-done = f32[2,256,512]{1,2,0:T(8,128)} collective-permute-done((f32[2,256,512]{1,2,0:T(8,128)}, f32[2,256,512]{1,2,0:T(8,128)}, u32[]{:S(2)}, u32[]{:S(2)}) %collective-permute-start) | collective-permute-done | bytes 1048608 | tf_op jit(solution)/shard_map/ppermute | solution.py:13
  252.3 18.3 %while.144 = (s32[]{:T(128)}, f32[2,32,64]{2,0,1:T(2,128)S(1)}, s32[]{:T(128)}, s32[]{:T(128)}, s32[]{:T(128)}, /*index=5*/s32[]{:T(128)}) while((s32[]{:T(128)}, f32[2,32,64]{2,0,1:T(2,128)S(1)}, s32[]{:T(128)}, s32[]{:T(128)}, s32[]{:T(128)}, /*index=5*/s32[]{:T(128)}) %tuple.349), condition=%wide.region_4.0_spmd.clone, body=%wide.region_2.0_spmd.clone.sunk | while | flops 20612 | bytes 43533 | solution.py:31
  274.3 3.2 fusion.16
  278.5 3.6 scatter.26
  283.0 18.3 %while.145 = (s32[]{:T(128)}, f32[2,32,64]{2,0,1:T(2,128)S(1)}, s32[]{:T(128)}, s32[]{:T(128)}, s32[]{:T(128)}, /*index=5*/s32[]{:T(128)}) while((s32[]{:T(128)}, f32[2,32,64]{2,0,1:T(2,128)S(1)}, s32[]{:T(128)}, s32[]{:T(128)}, s32[]{:T(128)}, /*index=5*/s32[]{:T(128)}) %tuple.352), condition=%wide.region_7.8_spmd.clone, body=%wide.region_5.7_spmd.clone.sunk | while | flops 20612 | bytes 43533 | solution.py:31
  303.1 3.3 convolution_subtract_fusion.6
  307.4 4.0 scatter.29
  312.4 18.3 %while.146 = (s32[]{:T(128)}, f32[2,32,64]{2,0,1:T(2,128)S(1)}, s32[]{:T(128)}, s32[]{:T(128)}, s32[]{:T(128)}, /*index=5*/s32[]{:T(128)}) while((s32[]{:T(128)}, f32[2,32,64]{2,0,1:T(2,128)S(1)}, s32[]{:T(128)}, s32[]{:T(128)}, s32[]{:T(128)}, /*index=5*/s32[]{:T(128)}) %tuple.355), condition=%wide.region_10.11_spmd.clone, body=%wide.region_8.10_spmd.clone.sunk | while | flops 20612 | bytes 43533 | solution.py:31
  332.5 3.4 convolution_subtract_fusion.5
  336.9 4.0 scatter.30
  341.9 18.3 %while.147 = (s32[]{:T(128)}, f32[2,32,64]{2,0,1:T(2,128)S(1)}, s32[]{:T(128)}, s32[]{:T(128)}, s32[]{:T(128)}, /*index=5*/s32[]{:T(128)}) while((s32[]{:T(128)}, f32[2,32,64]{2,0,1:T(2,128)S(1)}, s32[]{:T(128)}, s32[]{:T(128)}, s32[]{:T(128)}, /*index=5*/s32[]{:T(128)}) %tuple.358), condition=%wide.region_13.0_spmd.clone, body=%wide.region_11.13_spmd.clone.sunk | while | flops 20612 | bytes 43533 | solution.py:31
  362.0 3.3 convolution_subtract_fusion.4
  366.3 4.0 scatter.31
  371.2 18.3 %while.148 = (s32[]{:T(128)}, f32[2,32,64]{2,0,1:T(2,128)S(1)}, s32[]{:T(128)}, s32[]{:T(128)}, s32[]{:T(128)}, /*index=5*/s32[]{:T(128)}) while((s32[]{:T(128)}, f32[2,32,64]{2,0,1:T(2,128)S(1)}, s32[]{:T(128)}, s32[]{:T(128)}, s32[]{:T(128)}, /*index=5*/s32[]{:T(128)}) %tuple.361), condition=%wide.region_16.0_spmd.clone, body=%wide.region_14.0_spmd.clone.sunk | while | flops 20612 | bytes 43533 | solution.py:31
  391.2 3.4 convolution_subtract_fusion.3
  395.6 3.0 scatter.34
  399.5 18.5 %while.149 = (s32[]{:T(128)}, f32[2,32,64]{2,0,1:T(2,128)S(1)}, s32[]{:T(128)}, s32[]{:T(128)}, s32[]{:T(128)}, /*index=5*/s32[]{:T(128)}) while((s32[]{:T(128)}, f32[2,32,64]{2,0,1:T(2,128)S(1)}, s32[]{:T(128)}, s32[]{:T(128)}, s32[]{:T(128)}, /*index=5*/s32[]{:T(128)}) %tuple.364), condition=%wide.region_19.20_spmd.clone, body=%wide.region_17.19_spmd.clone.sunk | while | flops 20612 | bytes 43533 | solution.py:31
  419.8 3.3 convolution_subtract_fusion.2
  424.1 3.4 scatter.35
  428.5 18.3 %while.150 = (s32[]{:T(128)}, f32[2,32,64]{2,0,1:T(2,128)S(1)}, s32[]{:T(128)}, s32[]{:T(128)}, s32[]{:T(128)}, /*index=5*/s32[]{:T(128)}) while((s32[]{:T(128)}, f32[2,32,64]{2,0,1:T(2,128)S(1)}, s32[]{:T(128)}, s32[]{:T(128)}, s32[]{:T(128)}, /*index=5*/s32[]{:T(128)}) %tuple.367), condition=%wide.region_22.23_spmd.clone, body=%wide.region_20.22_spmd.clone.sunk | while | flops 20612 | bytes 43533 | solution.py:31
  448.6 3.4 convolution_subtract_fusion.1
  452.9 3.4 scatter.36
  457.2 18.3 %while.151 = (s32[]{:T(128)}, f32[2,32,64]{2,0,1:T(2,128)S(1)}, s32[]{:T(128)}, s32[]{:T(128)}, s32[]{:T(128)}, /*index=5*/s32[]{:T(128)}) while((s32[]{:T(128)}, f32[2,32,64]{2,0,1:T(2,128)S(1)}, s32[]{:T(128)}, s32[]{:T(128)}, s32[]{:T(128)}, /*index=5*/s32[]{:T(128)}) %tuple.370), condition=%wide.region_25.0_spmd.clone, body=%wide.region_23.25_spmd.clone.sunk | while | flops 20612 | bytes 43533 | solution.py:31
  477.3 3.3 convolution_subtract_fusion
  481.7 3.4 scatter.39
  485.1 2.5 convolution_subtract_fusion.7
  (1350 shorter events, 179.3 us)
Async XLA Ops:
  6.5 60.5 %copy-start = (f32[2,256,1024]{2,1,0:T(8,128)S(1)}, f32[2,256,1024]{2,1,0:T(8,128)}, u32[]{:S(2)}) copy-start(f32[2,256,1024]{2,1,0:T(8,128)} %param.36) | copy-start | bytes 6291460
  6.5 60.5 %all-gather.3.cloned.1.call-start = ((), (), s32[]{:S(2)}) async-start(), calls=%async_computation | async-start | bytes 2621440 | tf_op jit(solution)/shard_map/all_gather | solution.py:70
  7.3 114.5 %all-gather.5.cloned.1.call-start = ((), (), s32[]{:S(2)}) async-start(), calls=%async_computation.1 | async-start | bytes 2621440 | tf_op jit(solution)/shard_map/all_gather | solution.py:64
  8.0 62.7 %copy-start.2 = (f32[2,256,256]{2,1,0:T(8,128)S(1)}, f32[2,256,256]{2,1,0:T(8,128)}, u32[]{:S(2)}) copy-start(f32[2,256,256]{2,1,0:T(8,128)} %param.38) | copy-start | bytes 1572868
  8.0 188.9 %all-reduce.3.cloned.1.call-start = ((), (), s32[]{:S(2)}) async-start(), calls=%async_computation.2 | async-start | bytes 2097152 | tf_op jit(solution)/shard_map/psum | solution.py:75
  121.8 3.7 copy-start.3
  199.2 50.4 %collective-permute-start = (f32[2,256,512]{1,2,0:T(8,128)}, f32[2,256,512]{1,2,0:T(8,128)}, u32[]{:S(2)}, u32[]{:S(2)}) collective-permute-start(f32[2,256,512]{1,2,0:T(8,128)} %pad_maximum_fusion.1), channel_id=1, source_target_pairs={{0,16},{4,20},{8,24},{12,28},{16,0},{20,4},{24,8},{28,12},{32,48},... | collective-permute-start | bytes 3145736 | tf_op jit(solution)/shard_map/ppermute | solution.py:13
  251.4 0.8 copy-start.1
Sparse Core Ops, SparseCore 0:
  9.5 57.5 all-gather.2
  69.1 52.5 all-gather.4
  127.5 69.3 all-reduce.2
where the time goes:
time: 496 us; the launch traced here: 494 us
  waiting for transfers between devices  225 us (45%)
  other arithmetic  93.2 us (19%)
  local copies, waits for them, and re-layouts  91.9 us (19%)
  matrix products  58.1 us (12%)
  between operations  13.5 us (3%)
  loops' own time  7.86 us (2%)
    psum x1, waiting for transfers between devices, body(): own_g, own_h = lax.psum((partial_g, partial_h), 'col')  69.5 us
    all_gather x1, waiting for transfers between devices, body(): lax.all_gather(parent_gen, 'col', axis=1, tiled=True)  59 us
    all_gather x1, waiting for transfers between devices, body(): lax.all_gather(left_gen, 'col', axis=1, tiled=True)  49.2 us
    dynamic_slice x256, local copies, waits for them, and re-layouts, eliminate(): pivot = lax.dynamic_slice_in_dim(pivot_row, step, 1, 1)  47.8 us
    ppermute x1, waiting for transfers between devices, partner(): lax.ppermute(shard, axis, [(i, i ^ 1 << distance) for i in range(lax.axis...  45.5 us
    add x256, other arithmetic, eliminate(): return current + selector[None, :, None] * pivot_row[:, None, :]  41.5 us
    reduce_sum x256, other arithmetic, eliminate(): column = jnp.sum(current[:, :, :width] * selector[None, None, :], axis=2)  29.4 us
    scatter x8, local copies, waits for them, and re-layouts, block_solve(): joined = updated.at[:, start:finish, :].set(row_band)  28.9 us
  transfers between devices with their start and end apart: 4, of which 4 were waited for; matrix products, arithmetic and copies ran while one was open for 1% of the time, Pallas kernels for 0%

commit v1 on v0

v1 whole, which is shorter than its diff:
```python
import functools

import jax
import jax.numpy as jnp
from jax import lax
from jax.experimental import pallas as pl
from jax.experimental.pallas import tpu as pltpu
from jax.sharding import PartitionSpec as P

LEVEL = 2
RUN = 4
NN = (((1,), (0,)), ((), ()))
NT = (((1,), (1,)), ((), ()))
TN = (((0,), (0,)), ((), ()))
PARAMS = pltpu.CompilerParams(vmem_limit_bytes=40 * 1024 * 1024)
SETTLED = 2.4e-4
DOUBLINGS = 9


def split(value):
    high = value.astype(jnp.bfloat16)
    low = (value - high.astype(jnp.float32)).astype(jnp.bfloat16)
    return high, low


def dot3(left, right, dims=NN):
    product = functools.partial(
        lax.dot_general, dimension_numbers=dims, preferred_element_type=jnp.float32
    )
    (lh, ll), (rh, rl) = left, right
    return product(lh, rh) + (product(lh, rl) + product(ll, rh))


def mul(left, right, dims=NN):
    return dot3(split(left), split(right), dims)


def exact(left, right, dims=NN):
    return lax.dot_general(
        left, right, dims, precision=lax.Precision.HIGHEST, preferred_element_type=jnp.float32
    )


def apply_kernel(place, inverse, right, own, left0, right0, left1, right1, left2, right2, solved, small):
    c = place[0]
    rows = own.shape[1]
    inner = jnp.logical_and(c >= 1, c <= RUN - 2)
    for leaf in range(own.shape[0]):
        blocks = (
            (c, own[leaf]),
            (jnp.where(c >= 2, c - 2, c + 2), left1[leaf] + right1[leaf]),
            (jnp.where(c >= 1, c - 1, c + 1), jnp.where(c >= 1, left0[leaf], right0[leaf])),
            (
                jnp.where(inner, c + 1, RUN - 1 - c),
                jnp.where(inner, right0[leaf], left2[leaf] + right2[leaf]),
            ),
        )
        total = None
        for index, block in blocks:
            columns = pl.ds(pl.multiple_of(index * rows, rows), rows)
            term = mul(inverse[leaf, :, columns], block)
            total = term if total is None else total + term
        solved[leaf] = total
        small[leaf] = mul(total, right[leaf], TN)


def apply_gathered(place, inverse, right, blocks):
    own = blocks[0]
    leaves, rows, order_k = own.shape
    vmem = pl.BlockSpec(memory_space=pltpu.VMEM)
    return pl.pallas_call(
        apply_kernel,
        out_shape=(
            jax.ShapeDtypeStruct((leaves, inverse.shape[1], order_k), jnp.float32),
            jax.ShapeDtypeStruct((leaves, order_k, order_k), jnp.float32),
        ),
        in_specs=[pl.BlockSpec(memory_space=pltpu.SMEM)] + [vmem] * 9,
        out_specs=(vmem, vmem),
        compiler_params=PARAMS,
        cost_estimate=pl.CostEstimate(
            flops=10 * leaves * rows * order_k * rows * 3, bytes_accessed=6 << 20, transcendentals=0
        ),
        name="apply",
    )(place, inverse, right, *blocks)


def eliminate(matrix, joined):
    size = matrix.shape[0]
    row = lax.broadcasted_iota(jnp.int32, (size, size), 0)
    lane = lax.broadcasted_iota(jnp.int32, (size, size), 1)
    identity = (row == lane).astype(jnp.float32)
    joined[0] = matrix
    joined[1] = identity
    tall = lax.broadcasted_iota(jnp.int32, (size, 1), 0)

    def step(k, carry):
        used, picks = carry
        left = joined[0]
        column = jnp.sum(jnp.where(lane == k, left, 0.0), axis=1, keepdims=True)
        height = jnp.where(used > 0.0, -1.0, jnp.abs(column))
        best = jnp.max(height, axis=0, keepdims=True)
        pick = jnp.min(jnp.where(height == best, tall, size), axis=0, keepdims=True)
        chosen = tall == pick
        pivot = jnp.sum(jnp.where(chosen, column, 0.0), axis=0, keepdims=True)
        others = jnp.where(chosen, 0.0, column)
        for side in range(2):
            part = joined[side]
            pivot_row = jnp.sum(jnp.where(chosen, part, 0.0), axis=0, keepdims=True) / pivot
            joined[side] = jnp.where(chosen, pivot_row, part - others * pivot_row)
        picks = jnp.where(jnp.logical_and(chosen, lane == k), 1.0, picks)
        return jnp.where(chosen, 1.0, used), picks

    _, picks = lax.fori_loop(
        0, size, step, (jnp.zeros((size, 1), jnp.float32), jnp.zeros((size, size), jnp.float32))
    )
    return exact(picks, joined[1], TN)


def invert_kernel(gathered, inverse, power, joined):
    size = inverse.shape[0]
    first = gathered[:, 0].reshape(size, size)
    second = gathered[:, 1].reshape(size, size)
    row = lax.broadcasted_iota(jnp.int32, (size, size), 0)
    lane = lax.broadcasted_iota(jnp.int32, (size, size), 1)
    identity = (row == lane).astype(jnp.float32)
    start = exact(first, second)
    power[...] = start
    inverse[...] = identity + start

    def unsettled(state):
        count, norm = state
        going = jnp.logical_and(norm > SETTLED * SETTLED, norm < 1e12)
        return jnp.logical_and(count < DOUBLINGS, going)

    def double(state):
        count, _ = state
        current = split(power[...])
        square = dot3(current, current)
        power[...] = square
        held = inverse[...]
        inverse[...] = held + mul(held, square)
        return count + 1, jnp.sum(square * square)

    _, norm = lax.while_loop(unsettled, double, (jnp.int32(0), jnp.sum(start * start)))

    @pl.when(jnp.logical_not(norm <= SETTLED * SETTLED))
    def _():
        inverse[...] = eliminate(identity - exact(first, second), joined)


def invert(gathered):
    size = gathered.shape[-1]
    vmem = pl.BlockSpec(memory_space=pltpu.VMEM)
    return pl.pallas_call(
        invert_kernel,
        out_shape=jax.ShapeDtypeStruct((size, size), jnp.float32),
        in_specs=[vmem],
        out_specs=vmem,
        scratch_shapes=[
            pltpu.VMEM((size, size), jnp.float32),
            pltpu.VMEM((2, size, size), jnp.float32),
        ],
        compiler_params=PARAMS,
        cost_estimate=pl.CostEstimate(
            flops=10 * 6 * size**3, bytes_accessed=1 << 20, transcendentals=0
        ),
        name="invert",
    )(gathered)


def coeffs_kernel(pieces, gathered, inverse, sent):
    size = inverse.shape[0]
    first = gathered[:, 0].reshape(size, size)
    second = gathered[:, 1].reshape(size, size)
    first_h = pieces[0] + pieces[1] + (pieces[2] + pieces[3])
    second_h = pieces[4] + pieces[5] + (pieces[6] + pieces[7])
    target = second_h - mul(first_h, second)
    first_c = mul(target, inverse[...])
    second_c = first_h - mul(first_c, first)
    for q in range(RUN):
        sent[q] = first_c
        sent[RUN + q] = second_c


def coeffs(pieces, gathered, inverse):
    vmem = pl.BlockSpec(memory_space=pltpu.VMEM)
    return pl.pallas_call(
        coeffs_kernel,
        out_shape=jax.ShapeDtypeStruct(pieces.shape, jnp.float32),
        in_specs=[vmem] * 3,
        out_specs=vmem,
        compiler_params=PARAMS,
        name="coeffs",
    )(pieces, gathered, inverse)


def final_kernel(second, first, coeffs_t, out):
    for leaf in range(out.shape[0]):
        out[leaf] = second[leaf] - mul(first[leaf], coeffs_t[leaf], NT)


def final(second, first, coeffs_t):
    vmem = pl.BlockSpec(memory_space=pltpu.VMEM)
    return pl.pallas_call(
        final_kernel,
        out_shape=jax.ShapeDtypeStruct(second.shape, jnp.float32),
        in_specs=[vmem] * 3,
        out_specs=vmem,
        compiler_params=PARAMS,
        name="final",
    )(second, first, coeffs_t)


def hop(shard, direction, step):
    if direction > 0:
        pairs = [(i, i + 1) for i in range(step, RUN - 1)]
    else:
        pairs = [(i + 1, i) for i in range(0, RUN - 1 - step)]
    return lax.ppermute(shard, "col", pairs)


def body(leaf_inverse, left_gen, right_gen, parent_gen):
    leaves, rows, order_k = left_gen.shape
    quarter = order_k // RUN
    place = lax.axis_index("col").reshape(1).astype(jnp.int32)
    stride = 1 << LEVEL
    groups = [
        [side * RUN + q for side in (leaf, leaf ^ stride) for q in range(RUN)]
        for leaf in range(lax.axis_size("leaf"))
        if not leaf & stride
    ]

    def exchange(value):
        return lax.all_to_all(value, ("leaf", "col"), 0, 0, axis_index_groups=groups, tiled=True)

    def gather(own, after=None):
        blocks = [own]
        onward = back = own
        for step in range(RUN - 1):
            onward, back = hop(onward, 1, step), hop(back, -1, step)
            blocks += [onward, back]
        return blocks

    left_blocks = gather(left_gen)
    parent_start, _ = lax.optimization_barrier((parent_gen, left_blocks[3]))
    parent_blocks = gather(parent_start)

    first, small_g = apply_gathered(place, leaf_inverse, right_gen, left_blocks)
    pieces = exchange(small_g.reshape(2 * RUN, quarter, order_k))
    summed = jnp.sum(pieces.reshape(2, RUN, quarter, order_k), axis=1)
    gathered = lax.all_to_all(
        jnp.broadcast_to(summed, (RUN,) + summed.shape), "col", 0, 0, tiled=True
    )
    inverse = invert(gathered)

    second, small_h = apply_gathered(place, leaf_inverse, right_gen, parent_blocks)
    pieces_h = exchange(small_h.reshape(2 * RUN, quarter, order_k))
    sent = coeffs(pieces_h, gathered, inverse)
    coeffs_t = exchange(sent).reshape(leaves, order_k, order_k)
    return final(second, first, coeffs_t)


def solution(mesh):
    return jax.shard_map(
        body,
        mesh=mesh,
        in_specs=(
            P("leaf", "col", None),
            P("leaf", "col", None),
            P("leaf", "col", None),
            P("leaf", "col", None),
        ),
        out_specs=P("leaf", "col", None),
        check_vma=False,
    )
```

time: 496 us -> 162 us (0.33)
  waiting for transfers between devices: 225 us -> 79.7 us
  other arithmetic: 93.2 us -> 1.09 us
  local copies, waits for them, and re-layouts: 91.9 us -> 10.6 us
  matrix products: 58.1 us -> 0 us
  starting transfers between devices: 4.88 us -> 44.3 us
  blocking collectives: 0 us -> 14.6 us
  between operations: 13.5 us -> 0.21 us
  Pallas kernels: 0 us -> 10.9 us
  loops' own time: 7.86 us -> 0 us
    all_gather x2 -> x0, waiting for transfers between devices: 108 us -> none  [the longest x1 59 us: body(): lax.all_gather(parent_gen, 'col', axis=1, tiled=True)]
    psum x1 -> x0, waiting for transfers between devices: 69.5 us -> none  [body(): own_g, own_h = lax.psum((partial_g, partial_h), 'col')]
    dot_general x23 -> x0, matrix products: 58.1 us -> none  [the longest x8 26.7 us: block_solve(): jnp.einsum('lab,lbc->lac', column_band, row_band, precision=precise)]
    dynamic_slice x256 -> x0, local copies, waits for them, and re-layouts: 47.8 us -> none  [eliminate(): pivot = lax.dynamic_slice_in_dim(pivot_row, step, 1, 1)]
    add x256 -> x0, other arithmetic: 41.5 us -> none  [eliminate(): return current + selector[None, :, None] * pivot_row[:, None, :]]
    scatter x8 -> x0, local copies, waits for them, and re-layouts: 28.9 us -> none  [block_solve(): joined = updated.at[:, start:finish, :].set(row_band)]
    reduce_sum x256 -> x1, other arithmetic: 29.4 us -> 1.09 us  [body(): summed = jnp.sum(pieces.reshape(2, RUN, quarter, order_k), axis=1)]
    ppermute x1 -> x12, waiting for transfers between devices: 45.5 us -> 70.2 us  [hop(): return lax.ppermute(shard, 'col', pairs)]
  transfers between devices with their start and end apart: 4 -> 15, of which waited for: 4 -> 8; matrix products, arithmetic and copies ran while one was open for 1% -> 1% of each run, Pallas kernels for 0% -> 4%
where the time goes in v1:
time: 162 us; the launch traced here: 161 us
  waiting for transfers between devices  79.7 us (49%)
  starting transfers between devices  44.3 us (27%)
  blocking collectives  14.6 us (9%)
  Pallas kernels  10.9 us (7%)
  local copies, waits for them, and re-layouts  10.6 us (7%)
    ppermute x12, waiting for transfers between devices, hop(): return lax.ppermute(shard, 'col', pairs)  70.2 us
    ppermute x12, starting transfers between devices, hop(): return lax.ppermute(shard, 'col', pairs)  20.1 us
    all_to_all x1, blocking collectives, exchange(): lax.all_to_all(value, ('leaf', 'col'), 0, 0, axis_index_groups=groups, ti...  14.6 us
    all_to_all x2, starting transfers between devices, exchange(): lax.all_to_all(value, ('leaf', 'col'), 0, 0, axis_index_groups=groups, ti...  14.2 us
    all_to_all x1, starting transfers between devices, body(): lax.all_to_all(jnp.broadcast_to(summed, (RUN,) + summed.shape), 'col', 0,...  9.97 us
    unnamed x30, local copies, waits for them, and re-layouts  9.76 us
    all_to_all x2, waiting for transfers between devices, exchange(): lax.all_to_all(value, ('leaf', 'col'), 0, 0, axis_index_groups=groups, ti...  9.52 us
    pallas_call x2, Pallas kernels, apply_gathered(): pl.pallas_call(apply_kernel, out_shape=(jax.ShapeDtypeStruct((leaves, inv...  6.5 us
  transfers between devices with their start and end apart: 15, of which 8 were waited for; matrix products, arithmetic and copies ran while one was open for 1% of the time, Pallas kernels for 4%

profile of v1, /device:TPU:6, one launch (start us, length us, event | category | flops | bytes accessed | tf_op | source)
XLA Modules:
  0.0 161.4 jit_solution(17380411068560519424)
XLA Ops:
  0.0 3.5 %collective-permute-start = (f32[2,256,256]{2,1,0:T(8,128)}, f32[2,256,256]{2,1,0:T(8,128)S(1)}, u32[]{:S(2)}, u32[]{:S(2)}) collective-permute-start(f32[2,256,256]{2,1,0:T(8,128)} %own.2), channel_id=1, source_target_pairs={{0,1},{1,2},{2,3},{4,5},{5,6},{6,7},{8,9},{9,10},{10,11},{12,13},{... | collective-permute-start | bytes 1572872 | tf_op jit(solution)/shard_map/ppermute | solution.py:219
  3.5 1.3 collective-permute-start.8
  4.8 10.1 %collective-permute-done.left0 = f32[2,256,256]{2,1,0:T(8,128)S(1)} collective-permute-done((f32[2,256,256]{2,1,0:T(8,128)}, f32[2,256,256]{2,1,0:T(8,128)S(1)}, u32[]{:S(2)}, u32[]{:S(2)}) %collective-permute-start) | collective-permute-done | bytes 524320 | tf_op jit(solution)/shard_map/ppermute | solution.py:219
  15.6 3.3 %collective-permute-done.8.right0 = f32[2,256,256]{2,1,0:T(8,128)S(1)} collective-permute-done((f32[2,256,256]{2,1,0:T(8,128)}, f32[2,256,256]{2,1,0:T(8,128)S(1)}, u32[]{:S(2)}, u32[]{:S(2)}) %collective-permute-start.8) | collective-permute-done | bytes 524320 | tf_op jit(solution)/shard_map/ppermute | solution.py:219
  19.0 1.3 collective-permute-start.9
  21.0 12.5 %collective-permute-done.9.right1 = f32[2,256,256]{2,1,0:T(8,128)S(1)} collective-permute-done((f32[2,256,256]{2,1,0:T(8,128)S(1)}, f32[2,256,256]{2,1,0:T(8,128)S(1)}, u32[]{:S(2)}, u32[]{:S(2)}) %collective-permute-start.9) | collective-permute-done | bytes 524320 | tf_op jit(solution)/shard_map/ppermute | solution.py:219
  33.5 1.3 collective-permute-start.11
  34.8 12.3 %collective-permute-done.11.right2 = f32[2,256,256]{2,1,0:T(8,128)S(1)} collective-permute-done((f32[2,256,256]{2,1,0:T(8,128)S(1)}, f32[2,256,256]{2,1,0:T(8,128)S(1)}, u32[]{:S(2)}, u32[]{:S(2)}) %collective-permute-start.11) | collective-permute-done | bytes 524320 | tf_op jit(solution)/shard_map/ppermute | solution.py:219
  47.9 1.6 copy-done
  49.5 1.0 copy-done.2
  50.6 1.0 copy-done.4
  51.6 1.0 copy-done.8
  52.6 2.5 %apply.3 = (f32[2,256,256]{2,1,0:T(8,128)S(1)}, f32[2,256,256]{2,1,0:T(8,128)S(1)}) custom-call(s32[1]{0:T(128)} %bitcast.place, f32[2,256,1024]{2,1,0:T(8,128)S(1)} %copy-done, f32[2,256,256]{2,1,0:T(8,128)S(1)} %copy-done.2, f32[2,256,256]{2,1,0:T(8,128)S(1)} %copy-done.4, f32[2,256,256]{2,1,0:T(8,128)S(1)} %collective-permute-done.left0, ...), custom_call_target="tpu_custom_call" | custom-call | flops 1006632960 | bytes 6291456 | tf_op jit(solution)/shard_map/apply/pallas_call | solution.py:71
  56.8 5.8 %all-to-all-start.1 = ((f32[8,64,256]{2,1,0:T(8,128)}), f32[8,64,256]{2,1,0:T(8,128)}, u32[]{:S(2)}, u32[]{:S(2)}) async-start(f32[8,64,256]{2,1,0:T(8,128)} %bitcast.7), calls=%async_computation.1 | async-start | bytes 1048576 | tf_op jit(solution)/shard_map/all_to_all | solution.py:234
  62.6 1.3 collective-permute-start.3
  63.9 5.4 %collective-permute-start.2 = (f32[2,256,256]{2,1,0:T(8,128)S(1)}, f32[2,256,256]{2,1,0:T(8,128)}, u32[]{:S(2)}, u32[]{:S(2)}) collective-permute-start(f32[2,256,256]{2,1,0:T(8,128)S(1)} %copy-done.5), channel_id=1, source_target_pairs={{0,1},{1,2},{2,3},{4,5},{5,6},{6,7},{8,9},{9,10},{10,11},{12,13},{... | collective-permute-start | bytes 1572872 | tf_op jit(solution)/shard_map/ppermute | solution.py:219
  69.2 13.0 %collective-permute-done.3.right0 = f32[2,256,256]{2,1,0:T(8,128)} collective-permute-done((f32[2,256,256]{2,1,0:T(8,128)S(1)}, f32[2,256,256]{2,1,0:T(8,128)}, u32[]{:S(2)}, u32[]{:S(2)}) %collective-permute-start.3) | collective-permute-done | bytes 524320 | tf_op jit(solution)/shard_map/ppermute | solution.py:219
  82.3 1.3 collective-permute-start.5
  83.6 1.5 collective-permute-start.4
  85.0 1.1 bitcast_reduce_fusion
  86.1 0.8 broadcast_in_dim.3
  87.0 10.0 %all-to-all-start.2 = ((f32[4,2,64,256]{3,2,1,0:T(8,128)}), f32[4,2,64,256]{3,2,1,0:T(8,128)S(1)}, u32[]{:S(2)}, u32[]{:S(2)}) async-start(f32[4,2,64,256]{3,2,1,0:T(8,128)} %broadcast_in_dim.3), calls=%async_computation.2 | async-start | bytes 1048576 | tf_op jit(solution)/shard_map/all_to_all | solution.py:251
  96.9 3.5 %collective-permute-done.5.right1 = f32[2,256,256]{2,1,0:T(8,128)} collective-permute-done((f32[2,256,256]{2,1,0:T(8,128)}, f32[2,256,256]{2,1,0:T(8,128)}, u32[]{:S(2)}, u32[]{:S(2)}) %collective-permute-start.5) | collective-permute-done | bytes 524320 | tf_op jit(solution)/shard_map/ppermute | solution.py:219
  100.4 1.3 collective-permute-start.7
  102.4 15.3 %collective-permute-done.7.right2 = f32[2,256,256]{2,1,0:T(8,128)S(1)} collective-permute-done((f32[2,256,256]{2,1,0:T(8,128)}, f32[2,256,256]{2,1,0:T(8,128)S(1)}, u32[]{:S(2)}, u32[]{:S(2)}) %collective-permute-start.7) | collective-permute-done | bytes 524320 | tf_op jit(solution)/shard_map/ppermute | solution.py:219
  117.8 1.0 copy-done.6
  118.8 4.0 %apply.2 = (f32[2,256,256]{2,1,0:T(8,128)S(1)}, f32[2,256,256]{2,1,0:T(8,128)S(1)}) custom-call(s32[1]{0:T(128)} %bitcast.place, f32[2,256,1024]{2,1,0:T(8,128)S(1)} %copy-done.1, f32[2,256,256]{2,1,0:T(8,128)S(1)} %copy-done.3, f32[2,256,256]{2,1,0:T(8,128)S(1)} %copy-done.6, f32[2,256,256]{2,1,0:T(8,128)} %collective-permute-done.2.left0, ...), custom_call_target="tpu_custom_call" | custom-call | flops 1006632960 | bytes 6291456 | tf_op jit(solution)/shard_map/apply/pallas_call | solution.py:71
  124.5 8.4 %all-to-all-start = ((f32[8,64,256]{2,1,0:T(8,128)}), f32[8,64,256]{2,1,0:T(8,128)S(1)}, u32[]{:S(2)}, u32[]{:S(2)}) async-start(f32[8,64,256]{2,1,0:T(8,128)} %bitcast.8), calls=%async_computation | async-start | bytes 1048576 | tf_op jit(solution)/shard_map/all_to_all | solution.py:234
  132.9 2.5 %invert.1.inverse = f32[256,256]{1,0:T(8,128)S(1)} custom-call(f32[4,2,64,256]{3,2,1,0:T(8,128)S(1)} %all-to-all-done.2.gathered), custom_call_target="tpu_custom_call" | custom-call | flops 1006632960 | bytes 1048576 | tf_op jit(solution)/shard_map/invert/pallas_call | solution.py:154
  135.5 9.5 %all-to-all-done.pieces = f32[8,64,256]{2,1,0:T(8,128)S(1)} async-done(((f32[8,64,256]{2,1,0:T(8,128)}), f32[8,64,256]{2,1,0:T(8,128)S(1)}, u32[]{:S(2)}, u32[]{:S(2)}) %all-to-all-start) | async-done | bytes 524320 | tf_op jit(solution)/shard_map/all_to_all | solution.py:234
  145.6 14.6 %all_to_all.20 = f32[8,64,256]{2,1,0:T(8,128)S(1)} all-to-all(f32[8,64,256]{2,1,0:T(8,128)S(1)} %coeffs.1), channel_id=1, replica_groups={{0,1,2,3,16,17,18,19},{4,5,6,7,20,21,22,23},{8,9,10,11,24,25,26,27},{12..., dimensions={0} | all-to-all | bytes 1048576 | tf_op jit(solution)/shard_map/all_to_all | solution.py:234
  160.2 1.2 final.1
  (36 shorter events, 6.7 us)
Async XLA Ops:
  0.0 15.0 %collective-permute-start = (f32[2,256,256]{2,1,0:T(8,128)}, f32[2,256,256]{2,1,0:T(8,128)S(1)}, u32[]{:S(2)}, u32[]{:S(2)}) collective-permute-start(f32[2,256,256]{2,1,0:T(8,128)} %own.2), channel_id=1, source_target_pairs={{0,1},{1,2},{2,3},{4,5},{5,6},{6,7},{8,9},{9,10},{10,11},{12,13},{... | collective-permute-start | bytes 1572872 | tf_op jit(solution)/shard_map/ppermute | solution.py:219
  3.5 15.5 %collective-permute-start.8 = (f32[2,256,256]{2,1,0:T(8,128)}, f32[2,256,256]{2,1,0:T(8,128)S(1)}, u32[]{:S(2)}, u32[]{:S(2)}) collective-permute-start(f32[2,256,256]{2,1,0:T(8,128)} %own.2), channel_id=1, source_target_pairs={{1,0},{2,1},{3,2},{5,4},{6,5},{7,6},{9,8},{10,9},{11,10},{13,12},{... | collective-permute-start | bytes 1572872 | tf_op jit(solution)/shard_map/ppermute | solution.py:219
  15.0 5.3 %collective-permute-start.1 = (f32[2,256,256]{2,1,0:T(8,128)S(1)}, f32[2,256,256]{2,1,0:T(8,128)S(1)}, u32[]{:S(2)}, u32[]{:S(2)}) collective-permute-start(f32[2,256,256]{2,1,0:T(8,128)S(1)} %collective-permute-done.left0), channel_id=1, source_target_pairs={{1,2},{2,3},{5,6},{6,7},{9,10},{10,11},{13,14},{14,15},{17,18},{18... | collective-permute-start | bytes 1572872 | tf_op jit(solution)/shard_map/ppermute | solution.py:219
  19.0 14.5 %collective-permute-start.9 = (f32[2,256,256]{2,1,0:T(8,128)S(1)}, f32[2,256,256]{2,1,0:T(8,128)S(1)}, u32[]{:S(2)}, u32[]{:S(2)}) collective-permute-start(f32[2,256,256]{2,1,0:T(8,128)S(1)} %collective-permute-done.8.right0), channel_id=1, source_target_pairs={{1,0},{2,1},{5,4},{6,5},{9,8},{10,9},{13,12},{14,13},{17,16},{18,1... | collective-permute-start | bytes 1572872 | tf_op jit(solution)/shard_map/ppermute | solution.py:219
  20.3 14.5 %collective-permute-start.10 = (f32[2,256,256]{2,1,0:T(8,128)S(1)}, f32[2,256,256]{2,1,0:T(8,128)S(1)}, u32[]{:S(2)}, u32[]{:S(2)}) collective-permute-start(f32[2,256,256]{2,1,0:T(8,128)S(1)} %collective-permute-done.1.left1), channel_id=1, source_target_pairs={{2,3},{6,7},{10,11},{14,15},{18,19},{22,23},{26,27},{30,31},{34,35... | collective-permute-start | bytes 1572872 | tf_op jit(solution)/shard_map/ppermute | solution.py:219
  33.5 13.6 %collective-permute-start.11 = (f32[2,256,256]{2,1,0:T(8,128)S(1)}, f32[2,256,256]{2,1,0:T(8,128)S(1)}, u32[]{:S(2)}, u32[]{:S(2)}) collective-permute-start(f32[2,256,256]{2,1,0:T(8,128)S(1)} %collective-permute-done.9.right1), channel_id=1, source_target_pairs={{1,0},{5,4},{9,8},{13,12},{17,16},{21,20},{25,24},{29,28},{33,32},... | collective-permute-start | bytes 1572872 | tf_op jit(solution)/shard_map/ppermute | solution.py:219
  47.1 0.8 copy-start.7
  47.9 1.6 copy-start
  49.5 1.0 copy-start.2
  50.6 1.0 copy-start.4
  51.6 1.0 copy-start.8
  52.6 9.9 %copy-start.5 = (f32[2,256,256]{2,1,0:T(8,128)S(1)}, f32[2,256,256]{2,1,0:T(8,128)}, u32[]{:S(2)}) copy-start(f32[2,256,256]{2,1,0:T(8,128)} %own.1) | copy-start | bytes 1572868
  55.1 0.8 copy-start.9
  55.9 0.8 copy-start.11
  56.8 61.0 %copy-start.1 = (f32[2,256,1024]{2,1,0:T(8,128)S(1)}, f32[2,256,1024]{2,1,0:T(8,128)}, u32[]{:S(2)}) copy-start(f32[2,256,1024]{2,1,0:T(8,128)} %inverse.3) | copy-start | bytes 6291460
  56.8 61.0 %copy-start.3 = (f32[2,256,256]{2,1,0:T(8,128)S(1)}, f32[2,256,256]{2,1,0:T(8,128)}, u32[]{:S(2)}) copy-start(f32[2,256,256]{2,1,0:T(8,128)} %right.3) | copy-start | bytes 1572868
  56.8 28.3 %all-to-all-start.1 = ((f32[8,64,256]{2,1,0:T(8,128)}), f32[8,64,256]{2,1,0:T(8,128)}, u32[]{:S(2)}, u32[]{:S(2)}) async-start(f32[8,64,256]{2,1,0:T(8,128)} %bitcast.7), calls=%async_computation.1 | async-start | bytes 1048576 | tf_op jit(solution)/shard_map/all_to_all | solution.py:234
  62.6 19.7 %collective-permute-start.3 = (f32[2,256,256]{2,1,0:T(8,128)S(1)}, f32[2,256,256]{2,1,0:T(8,128)}, u32[]{:S(2)}, u32[]{:S(2)}) collective-permute-start(f32[2,256,256]{2,1,0:T(8,128)S(1)} %copy-done.5), channel_id=1, source_target_pairs={{1,0},{2,1},{3,2},{5,4},{6,5},{7,6},{9,8},{10,9},{11,10},{13,12},{... | collective-permute-start | bytes 1572872 | tf_op jit(solution)/shard_map/ppermute | solution.py:219
  63.9 19.7 %collective-permute-start.2 = (f32[2,256,256]{2,1,0:T(8,128)S(1)}, f32[2,256,256]{2,1,0:T(8,128)}, u32[]{:S(2)}, u32[]{:S(2)}) collective-permute-start(f32[2,256,256]{2,1,0:T(8,128)S(1)} %copy-done.5), channel_id=1, source_target_pairs={{0,1},{1,2},{2,3},{4,5},{5,6},{6,7},{8,9},{9,10},{10,11},{12,13},{... | collective-permute-start | bytes 1572872 | tf_op jit(solution)/shard_map/ppermute | solution.py:219
  82.3 18.2 %collective-permute-start.5 = (f32[2,256,256]{2,1,0:T(8,128)}, f32[2,256,256]{2,1,0:T(8,128)}, u32[]{:S(2)}, u32[]{:S(2)}) collective-permute-start(f32[2,256,256]{2,1,0:T(8,128)} %collective-permute-done.3.right0), channel_id=1, source_target_pairs={{1,0},{2,1},{5,4},{6,5},{9,8},{10,9},{13,12},{14,13},{17,16},{18,1... | collective-permute-start | bytes 1572872 | tf_op jit(solution)/shard_map/ppermute | solution.py:219
  83.6 18.2 %collective-permute-start.4 = (f32[2,256,256]{2,1,0:T(8,128)}, f32[2,256,256]{2,1,0:T(8,128)}, u32[]{:S(2)}, u32[]{:S(2)}) collective-permute-start(f32[2,256,256]{2,1,0:T(8,128)} %collective-permute-done.2.left0), channel_id=1, source_target_pairs={{1,2},{2,3},{5,6},{6,7},{9,10},{10,11},{13,14},{14,15},{17,18},{18... | collective-permute-start | bytes 1572872 | tf_op jit(solution)/shard_map/ppermute | solution.py:219
  87.0 37.5 %all-to-all-start.2 = ((f32[4,2,64,256]{3,2,1,0:T(8,128)}), f32[4,2,64,256]{3,2,1,0:T(8,128)S(1)}, u32[]{:S(2)}, u32[]{:S(2)}) async-start(f32[4,2,64,256]{3,2,1,0:T(8,128)} %broadcast_in_dim.3), calls=%async_computation.2 | async-start | bytes 1048576 | tf_op jit(solution)/shard_map/all_to_all | solution.py:251
  100.4 17.4 %collective-permute-start.7 = (f32[2,256,256]{2,1,0:T(8,128)}, f32[2,256,256]{2,1,0:T(8,128)S(1)}, u32[]{:S(2)}, u32[]{:S(2)}) collective-permute-start(f32[2,256,256]{2,1,0:T(8,128)} %collective-permute-done.5.right1), channel_id=1, source_target_pairs={{1,0},{5,4},{9,8},{13,12},{17,16},{21,20},{25,24},{29,28},{33,32},... | collective-permute-start | bytes 1572872 | tf_op jit(solution)/shard_map/ppermute | solution.py:219
  101.7 16.1 %collective-permute-start.6 = (f32[2,256,256]{2,1,0:T(8,128)}, f32[2,256,256]{2,1,0:T(8,128)S(1)}, u32[]{:S(2)}, u32[]{:S(2)}) collective-permute-start(f32[2,256,256]{2,1,0:T(8,128)} %collective-permute-done.4.left1), channel_id=1, source_target_pairs={{2,3},{6,7},{10,11},{14,15},{18,19},{22,23},{26,27},{30,31},{34,35... | collective-permute-start | bytes 1572872 | tf_op jit(solution)/shard_map/ppermute | solution.py:219
  117.8 1.0 copy-start.6
  122.9 0.8 copy-start.10
  123.7 0.8 copy-start.13
  124.5 20.5 %all-to-all-start = ((f32[8,64,256]{2,1,0:T(8,128)}), f32[8,64,256]{2,1,0:T(8,128)S(1)}, u32[]{:S(2)}, u32[]{:S(2)}) async-start(f32[8,64,256]{2,1,0:T(8,128)} %bitcast.8), calls=%async_computation | async-start | bytes 1048576 | tf_op jit(solution)/shard_map/all_to_all | solution.py:234
  135.4 24.7 %copy-start.12 = (f32[2,256,256]{2,1,0:T(8,128)S(1)}, f32[2,256,256]{2,1,0:T(8,128)}, u32[]{:S(2)}) copy-start(f32[2,256,256]{2,1,0:T(8,128)} %copy-done.11) | copy-start | bytes 1572868
  135.5 24.7 %copy-start.14 = (f32[2,256,256]{2,1,0:T(8,128)S(1)}, f32[2,256,256]{2,1,0:T(8,128)}, u32[]{:S(2)}) copy-start(f32[2,256,256]{2,1,0:T(8,128)} %copy-done.13) | copy-start | bytes 1572868

commit v2 on v1

--- a/solution.py
+++ b/solution.py
@@ -15,6 +15,7 @@
 PARAMS = pltpu.CompilerParams(vmem_limit_bytes=40 * 1024 * 1024)
 SETTLED = 2.4e-4
 DOUBLINGS = 9
+WEIGHT = 40
 
 
 def split(value):
@@ -41,47 +42,103 @@
     )
 
 
-def apply_kernel(place, inverse, right, own, left0, right0, left1, right1, left2, right2, solved, small):
+def near_kernel(place, inverse, own, left0, right0, left1, right1, partial, far_high, far_low):
     c = place[0]
     rows = own.shape[1]
     inner = jnp.logical_and(c >= 1, c <= RUN - 2)
+
+    def columns(index):
+        return pl.ds(pl.multiple_of(index * rows, rows), rows)
+
     for leaf in range(own.shape[0]):
-        blocks = (
-            (c, own[leaf]),
-            (jnp.where(c >= 2, c - 2, c + 2), left1[leaf] + right1[leaf]),
-            (jnp.where(c >= 1, c - 1, c + 1), jnp.where(c >= 1, left0[leaf], right0[leaf])),
-            (
-                jnp.where(inner, c + 1, RUN - 1 - c),
-                jnp.where(inner, right0[leaf], left2[leaf] + right2[leaf]),
-            ),
-        )
-        total = None
-        for index, block in blocks:
-            columns = pl.ds(pl.multiple_of(index * rows, rows), rows)
-            term = mul(inverse[leaf, :, columns], block)
-            total = term if total is None else total + term
+        total = mul(inverse[leaf, :, columns(c)], own[leaf])
+        second = jnp.where(c >= 2, c - 2, c + 2)
+        total += mul(inverse[leaf, :, columns(second)], left1[leaf] + right1[leaf])
+        third = jnp.where(c >= 1, c - 1, c + 1)
+        block = jnp.where(c >= 1, left0[leaf], right0[leaf])
+        total += mul(inverse[leaf, :, columns(third)], block)
+        partial[leaf] = total
+        far = inverse[leaf, :, columns(jnp.where(inner, c + 1, RUN - 1 - c))]
+        far_high[leaf], far_low[leaf] = split(far)
+
+    @pl.when(inner)
+    def _():
+        for leaf in range(own.shape[0]):
+            far = (far_high[leaf], far_low[leaf])
+            partial[leaf] += dot3(far, split(right0[leaf]))
+            far_high[leaf] = jnp.zeros_like(far_high[leaf])
+            far_low[leaf] = jnp.zeros_like(far_low[leaf])
+
+
+def near(place, inverse, blocks, weight=1):
+    leaves, rows, order_k = blocks[0].shape
+    vmem = pl.BlockSpec(memory_space=pltpu.VMEM)
+    return pl.pallas_call(
+        near_kernel,
+        out_shape=(
+            jax.ShapeDtypeStruct((leaves, rows, order_k), jnp.float32),
+            jax.ShapeDtypeStruct((leaves, rows, rows), jnp.bfloat16),
+            jax.ShapeDtypeStruct((leaves, rows, rows), jnp.bfloat16),
+        ),
+        in_specs=[pl.BlockSpec(memory_space=pltpu.SMEM)] + [vmem] * 6,
+        out_specs=(vmem,) * 3,
+        compiler_params=PARAMS,
+        cost_estimate=pl.CostEstimate(
+            flops=weight * 8 * leaves * rows * order_k * rows * 3,
+            bytes_accessed=6 << 20,
+            transcendentals=0,
+        ),
+        name="near",
+    )(place, inverse, *blocks)
+
+
+def far_kernel(partial, far_high, far_low, left2, right2, right, solved, small):
+    for leaf in range(partial.shape[0]):
+        block = left2[leaf] + right2[leaf]
+        total = partial[leaf] + dot3((far_high[leaf], far_low[leaf]), split(block))
         solved[leaf] = total
         small[leaf] = mul(total, right[leaf], TN)
 
 
-def apply_gathered(place, inverse, right, blocks):
-    own = blocks[0]
-    leaves, rows, order_k = own.shape
-    vmem = pl.BlockSpec(memory_space=pltpu.VMEM)
-    return pl.pallas_call(
-        apply_kernel,
+def far(partial, far_high, far_low, left2, right2, right, weight=1):
+    leaves, rows, order_k = partial.shape
+    vmem = pl.BlockSpec(memory_space=pltpu.VMEM)
+    return pl.pallas_call(
+        far_kernel,
         out_shape=(
-            jax.ShapeDtypeStruct((leaves, inverse.shape[1], order_k), jnp.float32),
+            jax.ShapeDtypeStruct(partial.shape, jnp.float32),
             jax.ShapeDtypeStruct((leaves, order_k, order_k), jnp.float32),
         ),
-        in_specs=[pl.BlockSpec(memory_space=pltpu.SMEM)] + [vmem] * 9,
-        out_specs=(vmem, vmem),
+        in_specs=[vmem] * 6,
+        out_specs=(vmem,) * 2,
         compiler_params=PARAMS,
         cost_estimate=pl.CostEstimate(
-            flops=10 * leaves * rows * order_k * rows * 3, bytes_accessed=6 << 20, transcendentals=0
-        ),
-        name="apply",
-    )(place, inverse, right, *blocks)
+            flops=weight * 4 * leaves * rows * order_k * rows * 3,
+            bytes_accessed=3 << 20,
+            transcendentals=0,
+        ),
+        name="far",
+    )(partial, far_high, far_low, left2, right2, right)
+
+
+def spread_kernel(pieces, sent):
+    for side in range(2):
+        p = RUN * side
+        total = pieces[p] + pieces[p + 1] + (pieces[p + 2] + pieces[p + 3])
+        for q in range(RUN):
+            sent[q, side] = total
+
+
+def spread(pieces):
+    vmem = pl.BlockSpec(memory_space=pltpu.VMEM)
+    return pl.pallas_call(
+        spread_kernel,
+        out_shape=jax.ShapeDtypeStruct((RUN, 2) + pieces.shape[1:], jnp.float32),
+        in_specs=[vmem],
+        out_specs=vmem,
+        compiler_params=PARAMS,
+        name="spread",
+    )(pieces)
 
 
 def eliminate(matrix, joined):
@@ -233,27 +290,25 @@
     def exchange(value):
         return lax.all_to_all(value, ("leaf", "col"), 0, 0, axis_index_groups=groups, tiled=True)
 
-    def gather(own, after=None):
-        blocks = [own]
-        onward = back = own
-        for step in range(RUN - 1):
-            onward, back = hop(onward, 1, step), hop(back, -1, step)
-            blocks += [onward, back]
-        return blocks
-
-    left_blocks = gather(left_gen)
-    parent_start, _ = lax.optimization_barrier((parent_gen, left_blocks[3]))
-    parent_blocks = gather(parent_start)
-
-    first, small_g = apply_gathered(place, leaf_inverse, right_gen, left_blocks)
+    def hops(onward, back, step):
+        return hop(onward, 1, step), hop(back, -1, step)
+
+    left0 = hops(left_gen, left_gen, 0)
+    parent0 = hops(parent_gen, parent_gen, 0)
+    left1 = hops(*left0, 1)
+    left1, parent0 = lax.optimization_barrier((left1, parent0))
+    left2 = hops(*left1, 2)
+    parent1 = hops(*parent0, 1)
+    partial, *far_columns = near(place, leaf_inverse, (left_gen, *left0, *left1))
+    first, small_g = far(partial, *far_columns, *left2, right_gen)
+    parent2 = hops(*parent1, 2)
+
     pieces = exchange(small_g.reshape(2 * RUN, quarter, order_k))
-    summed = jnp.sum(pieces.reshape(2, RUN, quarter, order_k), axis=1)
-    gathered = lax.all_to_all(
-        jnp.broadcast_to(summed, (RUN,) + summed.shape), "col", 0, 0, tiled=True
-    )
+    gathered = lax.all_to_all(spread(pieces), "col", 0, 0, tiled=True)
     inverse = invert(gathered)
 
-    second, small_h = apply_gathered(place, leaf_inverse, right_gen, parent_blocks)
+    partial_h, *far_columns = near(place, leaf_inverse, (parent_gen, *parent0, *parent1), WEIGHT)
+    second, small_h = far(partial_h, *far_columns, *parent2, right_gen, WEIGHT)
     pieces_h = exchange(small_h.reshape(2 * RUN, quarter, order_k))
     sent = coeffs(pieces_h, gathered, inverse)
     coeffs_t = exchange(sent).reshape(leaves, order_k, order_k)

time: 162 us -> 139 us (0.86)
  waiting for transfers between devices: 79.7 us -> 61.1 us
  starting transfers between devices: 44.3 us -> 36.7 us
  Pallas kernels: 10.9 us -> 14.8 us
  local copies, waits for them, and re-layouts: 10.6 us -> 6.75 us
  blocking collectives: 14.6 us -> 18.2 us
    ppermute x12, waiting for transfers between devices: 70.2 us -> 43.8 us  [hop(): return lax.ppermute(shard, 'col', pairs)]
    all_to_all x2, waiting for transfers between devices: 9.52 us -> 17.3 us  [exchange(): lax.all_to_all(value, ('leaf', 'col'), 0, 0, axis_index_groups=groups, ti...]
    all_to_all x1, starting transfers between devices: 9.97 us -> 3.47 us  [body(): gathered = lax.all_to_all(spread(pieces), 'col', 0, 0, tiled=True)]
    pallas_call x2 -> x5, Pallas kernels: 6.5 us -> 10.5 us  [the longest x2 5.04 us: far(): pl.pallas_call(far_kernel, out_shape=(jax.ShapeDtypeStruct(partial.shape,...]
    all_to_all x1, blocking collectives: 14.6 us -> 18.2 us  [exchange(): lax.all_to_all(value, ('leaf', 'col'), 0, 0, axis_index_groups=groups, ti...]
    unnamed x30 -> x24, local copies, waits for them, and re-layouts: 9.76 us -> 6.75 us
    all_to_all x2, starting transfers between devices: 14.2 us -> 11.6 us  [exchange(): lax.all_to_all(value, ('leaf', 'col'), 0, 0, axis_index_groups=groups, ti...]
  transfers between devices with their start and end apart: 15 -> 15, of which waited for: 8 -> 9; matrix products, arithmetic and copies ran while one was open for 1% -> 0% of each run, Pallas kernels for 4% -> 9%
where the time goes in v2:
time: 139 us; the launch traced here: 138 us
  waiting for transfers between devices  61.1 us (44%)
  starting transfers between devices  36.7 us (26%)
  blocking collectives  18.2 us (13%)
  Pallas kernels  14.8 us (11%)
  local copies, waits for them, and re-layouts  6.75 us (5%)
    ppermute x12, waiting for transfers between devices, hop(): return lax.ppermute(shard, 'col', pairs)  43.8 us
    ppermute x12, starting transfers between devices, hop(): return lax.ppermute(shard, 'col', pairs)  21.6 us
    all_to_all x1, blocking collectives, exchange(): lax.all_to_all(value, ('leaf', 'col'), 0, 0, axis_index_groups=groups, ti...  18.2 us
    all_to_all x2, waiting for transfers between devices, exchange(): lax.all_to_all(value, ('leaf', 'col'), 0, 0, axis_index_groups=groups, ti...  17.3 us
    all_to_all x2, starting transfers between devices, exchange(): lax.all_to_all(value, ('leaf', 'col'), 0, 0, axis_index_groups=groups, ti...  11.6 us
    unnamed x24, local copies, waits for them, and re-layouts  6.75 us
    pallas_call x2, Pallas kernels, far(): pl.pallas_call(far_kernel, out_shape=(jax.ShapeDtypeStruct(partial.shape,...  5.04 us
    pallas_call x2, Pallas kernels, near(): pl.pallas_call(near_kernel, out_shape=(jax.ShapeDtypeStruct((leaves, rows...  4.62 us
  transfers between devices with their start and end apart: 15, of which 9 were waited for; matrix products, arithmetic and copies ran while one was open for 0% of the time, Pallas kernels for 9%

profile of v2, /device:TPU:6, one launch (start us, length us, event | category | flops | bytes accessed | tf_op | source)
XLA Modules:
  0.0 137.8 jit_solution(7939993373157461186)
XLA Ops:
  0.0 3.5 %collective-permute-start = (f32[2,256,256]{2,1,0:T(8,128)}, f32[2,256,256]{2,1,0:T(8,128)S(1)}, u32[]{:S(2)}, u32[]{:S(2)}) collective-permute-start(f32[2,256,256]{2,1,0:T(8,128)} %own.3), channel_id=1, source_target_pairs={{0,1},{1,2},{2,3},{4,5},{5,6},{6,7},{8,9},{9,10},{10,11},{12,13},{... | collective-permute-start | bytes 1572872 | tf_op jit(solution)/shard_map/ppermute | solution.py:276
  3.5 1.3 collective-permute-start.2
  4.8 5.4 %collective-permute-start.4 = (f32[2,256,256]{2,1,0:T(8,128)}, f32[2,256,256]{2,1,0:T(8,128)}, u32[]{:S(2)}, u32[]{:S(2)}) collective-permute-start(f32[2,256,256]{2,1,0:T(8,128)} %own.2), channel_id=1, source_target_pairs={{0,1},{1,2},{2,3},{4,5},{5,6},{6,7},{8,9},{9,10},{10,11},{12,13},{... | collective-permute-start | bytes 1572872 | tf_op jit(solution)/shard_map/ppermute | solution.py:276
  10.2 1.3 collective-permute-start.5
  11.5 4.6 %collective-permute-done.left0 = f32[2,256,256]{2,1,0:T(8,128)S(1)} collective-permute-done((f32[2,256,256]{2,1,0:T(8,128)}, f32[2,256,256]{2,1,0:T(8,128)S(1)}, u32[]{:S(2)}, u32[]{:S(2)}) %collective-permute-start) | collective-permute-done | bytes 524320 | tf_op jit(solution)/shard_map/ppermute | solution.py:276
  16.8 3.7 %collective-permute-done.2.right0 = f32[2,256,256]{2,1,0:T(8,128)S(1)} collective-permute-done((f32[2,256,256]{2,1,0:T(8,128)}, f32[2,256,256]{2,1,0:T(8,128)S(1)}, u32[]{:S(2)}, u32[]{:S(2)}) %collective-permute-start.2) | collective-permute-done | bytes 524320 | tf_op jit(solution)/shard_map/ppermute | solution.py:276
  20.5 1.3 collective-permute-start.3
  21.8 4.4 %collective-permute-done.4.left0 = f32[2,256,256]{2,1,0:T(8,128)} collective-permute-done((f32[2,256,256]{2,1,0:T(8,128)}, f32[2,256,256]{2,1,0:T(8,128)}, u32[]{:S(2)}, u32[]{:S(2)}) %collective-permute-start.4) | collective-permute-done | bytes 524320 | tf_op jit(solution)/shard_map/ppermute | solution.py:276
  26.2 5.6 %collective-permute-done.5.right0 = f32[2,256,256]{2,1,0:T(8,128)} collective-permute-done((f32[2,256,256]{2,1,0:T(8,128)}, f32[2,256,256]{2,1,0:T(8,128)}, u32[]{:S(2)}, u32[]{:S(2)}) %collective-permute-start.5) | collective-permute-done | bytes 524320 | tf_op jit(solution)/shard_map/ppermute | solution.py:276
  31.8 9.8 %collective-permute-done.3.right1 = f32[2,256,256]{2,1,0:T(8,128)} collective-permute-done((f32[2,256,256]{2,1,0:T(8,128)S(1)}, f32[2,256,256]{2,1,0:T(8,128)}, u32[]{:S(2)}, u32[]{:S(2)}) %collective-permute-start.3) | collective-permute-done | bytes 524320 | tf_op jit(solution)/shard_map/ppermute | solution.py:276
  41.6 1.4 %collective-permute-start.10 = (f32[2,256,256]{2,1,0:T(8,128)S(1)}, f32[2,256,256]{2,1,0:T(8,128)}, u32[]{:S(2)}, u32[]{:S(2)}) collective-permute-start(f32[2,256,256]{2,1,0:T(8,128)S(1)} %collective-permute-done.1.left1), channel_id=1, source_target_pairs={{2,3},{6,7},{10,11},{14,15},{18,19},{22,23},{26,27},{30,31},{34,35... | collective-permute-start | bytes 1572872 | tf_op jit(solution)/shard_map/ppermute | solution.py:276
  43.0 1.3 collective-permute-start.11
  44.3 1.5 %collective-permute-start.6 = (f32[2,256,256]{2,1,0:T(8,128)}, f32[2,256,256]{2,1,0:T(8,128)}, u32[]{:S(2)}, u32[]{:S(2)}) collective-permute-start(f32[2,256,256]{2,1,0:T(8,128)} %collective-permute-done.4.left0), channel_id=1, source_target_pairs={{1,2},{2,3},{5,6},{6,7},{9,10},{10,11},{13,14},{14,15},{17,18},{18... | collective-permute-start | bytes 1572872 | tf_op jit(solution)/shard_map/ppermute | solution.py:276
  45.8 1.3 collective-permute-start.7
  47.1 1.6 %copy-done = f32[2,256,1024]{2,1,0:T(8,128)S(1)} copy-done((f32[2,256,1024]{2,1,0:T(8,128)S(1)}, f32[2,256,1024]{2,1,0:T(8,128)}, u32[]{:S(2)}) %copy-start) | copy-done | bytes 2097176
  48.7 1.0 copy-done.2
  49.7 2.1 %near.3 = (f32[2,256,256]{2,1,0:T(8,128)S(1)}, bf16[2,256,256]{2,1,0:T(8,128)(2,1)S(1)}, bf16[2,256,256]{2,1,0:T(8,128)(2,1)S(1)}) custom-call(s32[1]{0:T(128)} %bitcast.place, f32[2,256,1024]{2,1,0:T(8,128)S(1)} %copy-done, f32[2,256,256]{2,1,0:T(8,128)S(1)} %copy-done.2, f32[2,256,256]{2,1,0:T(8,128)S(1)} %collective-permute-done.left0, ...), custom_call_target="tpu_custom_call" | custom-call | flops 805306368 | bytes 6291456 | tf_op jit(solution)/shard_map/near/pallas_call | solution.py:76
  51.8 8.2 %collective-permute-done.11.right2 = f32[2,256,256]{2,1,0:T(8,128)} collective-permute-done((f32[2,256,256]{2,1,0:T(8,128)}, f32[2,256,256]{2,1,0:T(8,128)}, u32[]{:S(2)}, u32[]{:S(2)}) %collective-permute-start.11) | collective-permute-done | bytes 524320 | tf_op jit(solution)/shard_map/ppermute | solution.py:276
  60.1 2.1 %far.3 = (f32[2,256,256]{2,1,0:T(8,128)S(1)}, f32[2,256,256]{2,1,0:T(8,128)S(1)}) custom-call(f32[2,256,256]{2,1,0:T(8,128)S(1)} %get-tuple-element.27.partial, bf16[2,256,256]{2,1,0:T(8,128)(2,1)S(1)} %get-tuple-element.28.far_high, bf16[2,256,256]{2,1,0:T(8,128)(2,1)S(1)} %get-tuple-element.29.far_low, f32[2,256,256]{2,1,0:T(8,128)} %collective-permute-done.10.left2, ...), custom_call_target="tpu_custom_call" | custom-call | flops 402653184 | bytes 3145728 | tf_op jit(solution)/shard_map/far/pallas_call | solution.py:106
  63.8 5.5 %all-to-all-start.1 = ((f32[8,64,256]{2,1,0:T(8,128)}), f32[8,64,256]{2,1,0:T(8,128)S(1)}, u32[]{:S(2)}, u32[]{:S(2)}) async-start(f32[8,64,256]{2,1,0:T(8,128)} %bitcast.5), calls=%async_computation.1 | async-start | bytes 1048576 | tf_op jit(solution)/shard_map/all_to_all | solution.py:291
  69.3 1.5 %collective-permute-start.8 = (f32[2,256,256]{2,1,0:T(8,128)}, f32[2,256,256]{2,1,0:T(8,128)}, u32[]{:S(2)}, u32[]{:S(2)}) collective-permute-start(f32[2,256,256]{2,1,0:T(8,128)} %collective-permute-done.6.left1), channel_id=1, source_target_pairs={{2,3},{6,7},{10,11},{14,15},{18,19},{22,23},{26,27},{30,31},{34,35... | collective-permute-start | bytes 1572872 | tf_op jit(solution)/shard_map/ppermute | solution.py:276
  70.7 1.3 collective-permute-start.9
  73.1 2.5 %near.2 = (f32[2,256,256]{2,1,0:T(8,128)S(1)}, bf16[2,256,256]{2,1,0:T(8,128)(2,1)S(1)}, bf16[2,256,256]{2,1,0:T(8,128)(2,1)S(1)}) custom-call(s32[1]{0:T(128)} %bitcast.place, f32[2,256,1024]{2,1,0:T(8,128)S(1)} %copy-done.1, f32[2,256,256]{2,1,0:T(8,128)S(1)} %copy-done.7, f32[2,256,256]{2,1,0:T(8,128)} %collective-permute-done.4.left0, ...), custom_call_target="tpu_custom_call" | custom-call | flops 32212254720 | bytes 6291456 | tf_op jit(solution)/shard_map/near/pallas_call | solution.py:76
  77.1 6.1 %all-to-all-done.1.pieces = f32[8,64,256]{2,1,0:T(8,128)S(1)} async-done(((f32[8,64,256]{2,1,0:T(8,128)}), f32[8,64,256]{2,1,0:T(8,128)S(1)}, u32[]{:S(2)}, u32[]{:S(2)}) %all-to-all-start.1) | async-done | bytes 524320 | tf_op jit(solution)/shard_map/all_to_all | solution.py:291
  84.0 3.5 %all-to-all-start.2 = ((f32[4,2,64,256]{3,2,1,0:T(8,128)}), f32[4,2,64,256]{3,2,1,0:T(8,128)S(1)}, u32[]{:S(2)}, u32[]{:S(2)}) async-start(f32[4,2,64,256]{3,2,1,0:T(8,128)} %spread.1), calls=%async_computation.2 | async-start | bytes 1048576 | tf_op jit(solution)/shard_map/all_to_all | solution.py:307
  87.5 7.4 %collective-permute-done.9.right2 = f32[2,256,256]{2,1,0:T(8,128)} collective-permute-done((f32[2,256,256]{2,1,0:T(8,128)}, f32[2,256,256]{2,1,0:T(8,128)}, u32[]{:S(2)}, u32[]{:S(2)}) %collective-permute-start.9) | collective-permute-done | bytes 524320 | tf_op jit(solution)/shard_map/ppermute | solution.py:276
  94.9 2.9 %far.2 = (f32[2,256,256]{2,1,0:T(8,128)S(1)}, f32[2,256,256]{2,1,0:T(8,128)}) custom-call(f32[2,256,256]{2,1,0:T(8,128)S(1)} %copy-done.9, bf16[2,256,256]{2,1,0:T(8,128)(2,1)S(1)} %get-tuple-element.22.far_high, bf16[2,256,256]{2,1,0:T(8,128)(2,1)S(1)} %copy-done.11, f32[2,256,256]{2,1,0:T(8,128)} %collective-permute-done.8.left2, ...), custom_call_target="tpu_custom_call" | custom-call | flops 16106127360 | bytes 3145728 | tf_op jit(solution)/shard_map/far/pallas_call | solution.py:106
  97.9 6.1 %all-to-all-start = ((f32[8,64,256]{2,1,0:T(8,128)}), f32[8,64,256]{2,1,0:T(8,128)S(1)}, u32[]{:S(2)}, u32[]{:S(2)}) async-start(f32[8,64,256]{2,1,0:T(8,128)} %bitcast.1), calls=%async_computation | async-start | bytes 1048576 | tf_op jit(solution)/shard_map/all_to_all | solution.py:291
  104.0 2.5 %invert.1.inverse = f32[256,256]{1,0:T(8,128)S(1)} custom-call(f32[4,2,64,256]{3,2,1,0:T(8,128)S(1)} %all-to-all-done.2.gathered), custom_call_target="tpu_custom_call" | custom-call | flops 1006632960 | bytes 1048576 | tf_op jit(solution)/shard_map/invert/pallas_call | solution.py:211
  106.5 11.2 %all-to-all-done.pieces = f32[8,64,256]{2,1,0:T(8,128)S(1)} async-done(((f32[8,64,256]{2,1,0:T(8,128)}), f32[8,64,256]{2,1,0:T(8,128)S(1)}, u32[]{:S(2)}, u32[]{:S(2)}) %all-to-all-start) | async-done | bytes 524320 | tf_op jit(solution)/shard_map/all_to_all | solution.py:291
  118.4 18.2 %all_to_all.20 = f32[8,64,256]{2,1,0:T(8,128)S(1)} all-to-all(f32[8,64,256]{2,1,0:T(8,128)S(1)} %coeffs.1), channel_id=1, replica_groups={{0,1,2,3,16,17,18,19},{4,5,6,7,20,21,22,23},{8,9,10,11,24,25,26,27},{12..., dimensions={0} | all-to-all | bytes 1048576 | tf_op jit(solution)/shard_map/all_to_all | solution.py:291
  136.6 1.2 final.1
  (31 shorter events, 6.3 us)
Async XLA Ops:
  0.0 16.1 %collective-permute-start = (f32[2,256,256]{2,1,0:T(8,128)}, f32[2,256,256]{2,1,0:T(8,128)S(1)}, u32[]{:S(2)}, u32[]{:S(2)}) collective-permute-start(f32[2,256,256]{2,1,0:T(8,128)} %own.3), channel_id=1, source_target_pairs={{0,1},{1,2},{2,3},{4,5},{5,6},{6,7},{8,9},{9,10},{10,11},{12,13},{... | collective-permute-start | bytes 1572872 | tf_op jit(solution)/shard_map/ppermute | solution.py:276
  3.5 17.0 %collective-permute-start.2 = (f32[2,256,256]{2,1,0:T(8,128)}, f32[2,256,256]{2,1,0:T(8,128)S(1)}, u32[]{:S(2)}, u32[]{:S(2)}) collective-permute-start(f32[2,256,256]{2,1,0:T(8,128)} %own.3), channel_id=1, source_target_pairs={{1,0},{2,1},{3,2},{5,4},{6,5},{7,6},{9,8},{10,9},{11,10},{13,12},{... | collective-permute-start | bytes 1572872 | tf_op jit(solution)/shard_map/ppermute | solution.py:276
  4.8 21.4 %collective-permute-start.4 = (f32[2,256,256]{2,1,0:T(8,128)}, f32[2,256,256]{2,1,0:T(8,128)}, u32[]{:S(2)}, u32[]{:S(2)}) collective-permute-start(f32[2,256,256]{2,1,0:T(8,128)} %own.2), channel_id=1, source_target_pairs={{0,1},{1,2},{2,3},{4,5},{5,6},{6,7},{8,9},{9,10},{10,11},{12,13},{... | collective-permute-start | bytes 1572872 | tf_op jit(solution)/shard_map/ppermute | solution.py:276
  10.2 21.6 %collective-permute-start.5 = (f32[2,256,256]{2,1,0:T(8,128)}, f32[2,256,256]{2,1,0:T(8,128)}, u32[]{:S(2)}, u32[]{:S(2)}) collective-permute-start(f32[2,256,256]{2,1,0:T(8,128)} %own.2), channel_id=1, source_target_pairs={{1,0},{2,1},{3,2},{5,4},{6,5},{7,6},{9,8},{10,9},{11,10},{13,12},{... | collective-permute-start | bytes 1572872 | tf_op jit(solution)/shard_map/ppermute | solution.py:276
  16.1 15.7 %collective-permute-start.1 = (f32[2,256,256]{2,1,0:T(8,128)S(1)}, f32[2,256,256]{2,1,0:T(8,128)S(1)}, u32[]{:S(2)}, u32[]{:S(2)}) collective-permute-start(f32[2,256,256]{2,1,0:T(8,128)S(1)} %collective-permute-done.left0), channel_id=1, source_target_pairs={{1,2},{2,3},{5,6},{6,7},{9,10},{10,11},{13,14},{14,15},{17,18},{18... | collective-permute-start | bytes 1572872 | tf_op jit(solution)/shard_map/ppermute | solution.py:276
  20.5 21.1 %collective-permute-start.3 = (f32[2,256,256]{2,1,0:T(8,128)S(1)}, f32[2,256,256]{2,1,0:T(8,128)}, u32[]{:S(2)}, u32[]{:S(2)}) collective-permute-start(f32[2,256,256]{2,1,0:T(8,128)S(1)} %collective-permute-done.2.right0), channel_id=1, source_target_pairs={{1,0},{2,1},{5,4},{6,5},{9,8},{10,9},{13,12},{14,13},{17,16},{18,1... | collective-permute-start | bytes 1572872 | tf_op jit(solution)/shard_map/ppermute | solution.py:276
  41.6 10.3 %collective-permute-start.10 = (f32[2,256,256]{2,1,0:T(8,128)S(1)}, f32[2,256,256]{2,1,0:T(8,128)}, u32[]{:S(2)}, u32[]{:S(2)}) collective-permute-start(f32[2,256,256]{2,1,0:T(8,128)S(1)} %collective-permute-done.1.left1), channel_id=1, source_target_pairs={{2,3},{6,7},{10,11},{14,15},{18,19},{22,23},{26,27},{30,31},{34,35... | collective-permute-start | bytes 1572872 | tf_op jit(solution)/shard_map/ppermute | solution.py:276
  43.0 17.1 %collective-permute-start.11 = (f32[2,256,256]{2,1,0:T(8,128)}, f32[2,256,256]{2,1,0:T(8,128)}, u32[]{:S(2)}, u32[]{:S(2)}) collective-permute-start(f32[2,256,256]{2,1,0:T(8,128)} %collective-permute-done.3.right1), channel_id=1, source_target_pairs={{1,0},{5,4},{9,8},{13,12},{17,16},{21,20},{25,24},{29,28},{33,32},... | collective-permute-start | bytes 1572872 | tf_op jit(solution)/shard_map/ppermute | solution.py:276
  44.3 25.0 %collective-permute-start.6 = (f32[2,256,256]{2,1,0:T(8,128)}, f32[2,256,256]{2,1,0:T(8,128)}, u32[]{:S(2)}, u32[]{:S(2)}) collective-permute-start(f32[2,256,256]{2,1,0:T(8,128)} %collective-permute-done.4.left0), channel_id=1, source_target_pairs={{1,2},{2,3},{5,6},{6,7},{9,10},{10,11},{13,14},{14,15},{17,18},{18... | collective-permute-start | bytes 1572872 | tf_op jit(solution)/shard_map/ppermute | solution.py:276
  45.8 25.0 %collective-permute-start.7 = (f32[2,256,256]{2,1,0:T(8,128)}, f32[2,256,256]{2,1,0:T(8,128)}, u32[]{:S(2)}, u32[]{:S(2)}) collective-permute-start(f32[2,256,256]{2,1,0:T(8,128)} %collective-permute-done.5.right0), channel_id=1, source_target_pairs={{1,0},{2,1},{5,4},{6,5},{9,8},{10,9},{13,12},{14,13},{17,16},{18,1... | collective-permute-start | bytes 1572872 | tf_op jit(solution)/shard_map/ppermute | solution.py:276
  47.1 1.6 %copy-start = (f32[2,256,1024]{2,1,0:T(8,128)S(1)}, f32[2,256,1024]{2,1,0:T(8,128)}, u32[]{:S(2)}) copy-start(f32[2,256,1024]{2,1,0:T(8,128)} %inverse.3) | copy-start | bytes 6291460
  48.7 1.0 copy-start.2
  49.7 10.4 %copy-start.3 = (f32[2,256,256]{2,1,0:T(8,128)S(1)}, f32[2,256,256]{2,1,0:T(8,128)}, u32[]{:S(2)}) copy-start(f32[2,256,256]{2,1,0:T(8,128)} %right.3) | copy-start | bytes 1572868
  51.8 20.2 %copy-start.1 = (f32[2,256,1024]{2,1,0:T(8,128)S(1)}, f32[2,256,1024]{2,1,0:T(8,128)}, u32[]{:S(2)}) copy-start(f32[2,256,1024]{2,1,0:T(8,128)} %inverse.3) | copy-start | bytes 6291460
  62.2 0.8 copy-start.5
  63.0 0.8 copy-start.4
  63.8 19.4 %all-to-all-start.1 = ((f32[8,64,256]{2,1,0:T(8,128)}), f32[8,64,256]{2,1,0:T(8,128)S(1)}, u32[]{:S(2)}, u32[]{:S(2)}) async-start(f32[8,64,256]{2,1,0:T(8,128)} %bitcast.5), calls=%async_computation.1 | async-start | bytes 1048576 | tf_op jit(solution)/shard_map/all_to_all | solution.py:291
  69.3 18.2 %collective-permute-start.8 = (f32[2,256,256]{2,1,0:T(8,128)}, f32[2,256,256]{2,1,0:T(8,128)}, u32[]{:S(2)}, u32[]{:S(2)}) collective-permute-start(f32[2,256,256]{2,1,0:T(8,128)} %collective-permute-done.6.left1), channel_id=1, source_target_pairs={{2,3},{6,7},{10,11},{14,15},{18,19},{22,23},{26,27},{30,31},{34,35... | collective-permute-start | bytes 1572872 | tf_op jit(solution)/shard_map/ppermute | solution.py:276
  70.7 24.2 %collective-permute-start.9 = (f32[2,256,256]{2,1,0:T(8,128)}, f32[2,256,256]{2,1,0:T(8,128)}, u32[]{:S(2)}, u32[]{:S(2)}) collective-permute-start(f32[2,256,256]{2,1,0:T(8,128)} %collective-permute-done.7.right1), channel_id=1, source_target_pairs={{1,0},{5,4},{9,8},{13,12},{17,16},{21,20},{25,24},{29,28},{33,32},... | collective-permute-start | bytes 1572872 | tf_op jit(solution)/shard_map/ppermute | solution.py:276
  72.0 1.0 copy-start.7
  75.6 0.8 copy-start.8
  76.4 0.7 copy-start.10
  83.2 11.8 %copy-start.9 = (f32[2,256,256]{2,1,0:T(8,128)S(1)}, f32[2,256,256]{2,1,0:T(8,128)}, u32[]{:S(2)}) copy-start(f32[2,256,256]{2,1,0:T(8,128)} %copy-done.8) | copy-start | bytes 1572868
  83.2 11.8 %copy-start.11 = (bf16[2,256,256]{2,1,0:T(8,128)(2,1)S(1)}, bf16[2,256,256]{2,1,0:T(8,128)(2,1)}, u32[]{:S(2)}) copy-start(bf16[2,256,256]{2,1,0:T(8,128)(2,1)} %copy-done.10) | copy-start | bytes 786436
  84.0 13.8 %all-to-all-start.2 = ((f32[4,2,64,256]{3,2,1,0:T(8,128)}), f32[4,2,64,256]{3,2,1,0:T(8,128)S(1)}, u32[]{:S(2)}, u32[]{:S(2)}) async-start(f32[4,2,64,256]{3,2,1,0:T(8,128)} %spread.1), calls=%async_computation.2 | async-start | bytes 1048576 | tf_op jit(solution)/shard_map/all_to_all | solution.py:307
  97.9 19.9 %all-to-all-start = ((f32[8,64,256]{2,1,0:T(8,128)}), f32[8,64,256]{2,1,0:T(8,128)S(1)}, u32[]{:S(2)}, u32[]{:S(2)}) async-start(f32[8,64,256]{2,1,0:T(8,128)} %bitcast.1), calls=%async_computation | async-start | bytes 1048576 | tf_op jit(solution)/shard_map/all_to_all | solution.py:291
  106.5 30.0 %copy-start.6 = (f32[2,256,256]{2,1,0:T(8,128)S(1)}, f32[2,256,256]{2,1,0:T(8,128)}, u32[]{:S(2)}) copy-start(f32[2,256,256]{2,1,0:T(8,128)} %copy-done.5) | copy-start | bytes 1572868

commit v3 on v1

v3 whole, which is shorter than its diff:
```python
import functools

import jax
import jax.numpy as jnp
from jax import lax
from jax.experimental import pallas as pl
from jax.experimental.pallas import tpu as pltpu
from jax.sharding import PartitionSpec as P

LEVEL = 2
RUN = 4
NN = (((1,), (0,)), ((), ()))
NT = (((1,), (1,)), ((), ()))
TN = (((0,), (0,)), ((), ()))
PARAMS = pltpu.CompilerParams(vmem_limit_bytes=16 * 1024 * 1024)
SETTLED = 2.4e-4
DOUBLINGS = 9
WEIGHT = 40


def split(value):
    high = value.astype(jnp.bfloat16)
    low = (value - high.astype(jnp.float32)).astype(jnp.bfloat16)
    return high, low


def dot3(left, right, dims=NN):
    product = functools.partial(
        lax.dot_general, dimension_numbers=dims, preferred_element_type=jnp.float32
    )
    (lh, ll), (rh, rl) = left, right
    return product(lh, rh) + (product(lh, rl) + product(ll, rh))


def mul(left, right, dims=NN):
    return dot3(split(left), split(right), dims)


def exact(left, right, dims=NN):
    return lax.dot_general(
        left, right, dims, precision=lax.Precision.HIGHEST, preferred_element_type=jnp.float32
    )


def call(kernel, name, shapes, operands, flops, scalars=0, scratch=()):
    vmem = pl.BlockSpec(memory_space=pltpu.VMEM)
    smem = pl.BlockSpec(memory_space=pltpu.SMEM)
    return pl.pallas_call(
        kernel,
        out_shape=tuple(jax.ShapeDtypeStruct(shape, dtype) for shape, dtype in shapes),
        in_specs=[smem] * scalars + [vmem] * (len(operands) - scalars),
        out_specs=(vmem,) * len(shapes),
        scratch_shapes=list(scratch),
        compiler_params=PARAMS,
        cost_estimate=pl.CostEstimate(flops=flops, bytes_accessed=4 << 20, transcendentals=0),
        name=name,
    )(*operands)


def block_columns(c, rows):
    near_half = c < RUN // 2
    indices = (c, jnp.bitwise_xor(c, 1), jnp.where(near_half, 2, 1), jnp.where(near_half, 3, 0))
    return [pl.ds(pl.multiple_of(index * rows, rows), rows) for index in indices]


def near_kernel(place, inverse, own, inner0, end0, across0, end1, part, far_high, far_low):
    strips = block_columns(place[0], own.shape[1])
    for leaf in range(own.shape[0]):
        total = mul(inverse[leaf, :, strips[0]], own[leaf])
        total += mul(inverse[leaf, :, strips[1]], inner0[leaf] + end0[leaf])
        part[leaf] = total + mul(inverse[leaf, :, strips[2]], across0[leaf] + end1[leaf])
        far_high[leaf], far_low[leaf] = split(inverse[leaf, :, strips[3]])


def last_kernel(part, far_high, far_low, across1, end2, right, solved, small):
    for leaf in range(part.shape[0]):
        block = split(across1[leaf] + end2[leaf])
        total = part[leaf] + dot3((far_high[leaf], far_low[leaf]), block)
        solved[leaf] = total
        small[leaf] = mul(total, right[leaf], TN)


def spread_kernel(pieces, sent):
    for side in range(2):
        p = RUN * side
        total = pieces[p] + pieces[p + 1] + (pieces[p + 2] + pieces[p + 3])
        for q in range(RUN):
            sent[q, side] = total


def eliminate(matrix, joined):
    size = matrix.shape[0]
    row = lax.broadcasted_iota(jnp.int32, (size, size), 0)
    lane = lax.broadcasted_iota(jnp.int32, (size, size), 1)
    identity = (row == lane).astype(jnp.float32)
    joined[0] = matrix
    joined[1] = identity
    tall = lax.broadcasted_iota(jnp.int32, (size, 1), 0)

    def step(k, carry):
        used, picks = carry
        left = joined[0]
        column = jnp.sum(jnp.where(lane == k, left, 0.0), axis=1, keepdims=True)
        height = jnp.where(used > 0.0, -1.0, jnp.abs(column))
        best = jnp.max(height, axis=0, keepdims=True)
        pick = jnp.min(jnp.where(height == best, tall, size), axis=0, keepdims=True)
        chosen = tall == pick
        pivot = jnp.sum(jnp.where(chosen, column, 0.0), axis=0, keepdims=True)
        others = jnp.where(chosen, 0.0, column)
        for side in range(2):
            part = joined[side]
            pivot_row = jnp.sum(jnp.where(chosen, part, 0.0), axis=0, keepdims=True) / pivot
            joined[side] = jnp.where(chosen, pivot_row, part - others * pivot_row)
        picks = jnp.where(jnp.logical_and(chosen, lane == k), 1.0, picks)
        return jnp.where(chosen, 1.0, used), picks

    _, picks = lax.fori_loop(
        0, size, step, (jnp.zeros((size, 1), jnp.float32), jnp.zeros((size, size), jnp.float32))
    )
    return exact(picks, joined[1], TN)


def invert_kernel(gathered, inverse, power, joined):
    size = inverse.shape[0]
    first = gathered[:, 0].reshape(size, size)
    second = gathered[:, 1].reshape(size, size)
    row = lax.broadcasted_iota(jnp.int32, (size, size), 0)
    lane = lax.broadcasted_iota(jnp.int32, (size, size), 1)
    identity = (row == lane).astype(jnp.float32)
    start = exact(first, second)
    power[...] = start
    inverse[...] = identity + start

    def unsettled(state):
        count, norm = state
        going = jnp.logical_and(norm > SETTLED * SETTLED, norm < 1e12)
        return jnp.logical_and(count < DOUBLINGS, going)

    def double(state):
        count, _ = state
        current = split(power[...])
        square = dot3(current, current)
        power[...] = square
        held = inverse[...]
        inverse[...] = held + mul(held, square)
        return count + 1, jnp.sum(square * square)

    _, norm = lax.while_loop(unsettled, double, (jnp.int32(0), jnp.sum(start * start)))

    @pl.when(jnp.logical_not(norm <= SETTLED * SETTLED))
    def _():
        inverse[...] = eliminate(identity - exact(first, second), joined)


def coeffs_kernel(pieces, gathered, inverse, sent):
    size = inverse.shape[0]
    first = gathered[:, 0].reshape(size, size)
    second = gathered[:, 1].reshape(size, size)
    first_h = pieces[0] + pieces[1] + (pieces[2] + pieces[3])
    second_h = pieces[4] + pieces[5] + (pieces[6] + pieces[7])
    target = second_h - mul(first_h, second)
    first_c = mul(target, inverse[...])
    second_c = first_h - mul(first_c, first)
    for q in range(RUN):
        sent[q] = first_c
        sent[RUN + q] = second_c


def final_kernel(second, first, coeffs_t, out):
    for leaf in range(out.shape[0]):
        out[leaf] = second[leaf] - mul(first[leaf], coeffs_t[leaf], NT)


TO_INNER = [(0, 1), (RUN - 1, RUN - 2)]
TO_END = [(1, 0), (RUN - 2, RUN - 1)]
ACROSS = [(1, RUN - 2), (RUN - 2, 1)]


def move(shard, pairs):
    return lax.ppermute(shard, "col", pairs)


def body(leaf_inverse, left_gen, right_gen, parent_gen):
    leaves, rows, order_k = left_gen.shape
    quarter = order_k // RUN
    place = lax.axis_index("col").reshape(1).astype(jnp.int32)
    stride = 1 << LEVEL
    groups = [
        [side * RUN + q for side in (leaf, leaf ^ stride) for q in range(RUN)]
        for leaf in range(lax.axis_size("leaf"))
        if not leaf & stride
    ]
    f32, bf16 = jnp.float32, jnp.bfloat16
    both = ((leaves, rows, order_k), f32)
    small = ((leaves, order_k, order_k), f32)
    strips = ((leaves, rows, rows), bf16)
    square = ((order_k, order_k), f32)
    unit = 6 * rows * rows * order_k

    def exchange(value):
        return lax.all_to_all(value, ("leaf", "col"), 0, 0, axis_index_groups=groups, tiled=True)

    def near(weight, *gens):
        return call(
            near_kernel,
            "near",
            (both, strips, strips),
            (place, leaf_inverse) + gens,
            weight * 6 * unit,
            scalars=1,
        )

    def last(weight, parts, *gens):
        return call(
            last_kernel, "last", (both, small), (*parts, *gens, right_gen), weight * 4 * unit
        )

    inner0 = move(left_gen, TO_INNER)
    across0 = move(left_gen, ACROSS)
    end0 = move(left_gen, TO_END)
    inner0, across0, end0, parent = lax.optimization_barrier((inner0, across0, end0, parent_gen))
    across1 = move(inner0, ACROSS)
    end1 = move(across0, TO_END)
    inner0_p = move(parent, TO_INNER)
    across1, end1, parent = lax.optimization_barrier((across1, end1, parent))
    end2 = move(across1, TO_END)
    across0_p = move(parent, ACROSS)
    end0_p = move(parent, TO_END)
    near_g = near(1, left_gen, inner0, end0, across0, end1)
    first, small_g = last(1, near_g, across1, end2)

    across1_p = move(inner0_p, ACROSS)
    end1_p = move(across0_p, TO_END)
    end2_p = move(across1_p, TO_END)
    near_h = near(WEIGHT, parent_gen, inner0_p, end0_p, across0_p, end1_p)
    second, small_h = last(WEIGHT, near_h, across1_p, end2_p)

    pieces = exchange(small_g.reshape(2 * RUN, quarter, order_k))
    (spread,) = call(
        spread_kernel, "spread", (((RUN, 2, quarter, order_k), f32),), (pieces,), unit // 8
    )
    gathered = lax.all_to_all(spread, "col", 0, 0, tiled=True)
    (inverse,) = call(
        invert_kernel,
        "invert",
        (square,),
        (gathered,),
        10 * unit,
        scratch=(pltpu.VMEM(square[0], f32), pltpu.VMEM((2,) + square[0], f32)),
    )
    pieces_h = exchange(small_h.reshape(2 * RUN, quarter, order_k))
    (sent,) = call(
        coeffs_kernel, "coeffs", ((pieces_h.shape, f32),), (pieces_h, gathered, inverse), unit
    )
    coeffs_t = exchange(sent).reshape(leaves, order_k, order_k)
    (out,) = call(final_kernel, "final", (both,), (second, first, coeffs_t), 2 * unit)
    return out


def solution(mesh):
    return jax.shard_map(
        body,
        mesh=mesh,
        in_specs=(
            P("leaf", "col", None),
            P("leaf", "col", None),
            P("leaf", "col", None),
            P("leaf", "col", None),
        ),
        out_specs=P("leaf", "col", None),
        check_vma=False,
    )
```

time: 162 us -> 137 us (0.85)
  waiting for transfers between devices: 79.7 us -> 60.9 us
  starting transfers between devices: 44.3 us -> 40.3 us
  local copies, waits for them, and re-layouts: 10.6 us -> 6.81 us
  Pallas kernels: 10.9 us -> 13.6 us
    ppermute x12, waiting for transfers between devices: 70.2 us -> 47 us  [move(): return lax.ppermute(shard, 'col', pairs)]
    all_to_all x1, starting transfers between devices: 9.97 us -> 3.47 us  [body(): gathered = lax.all_to_all(spread, 'col', 0, 0, tiled=True)]
    all_to_all x1, waiting for transfers between devices: 0.01 us -> 3.02 us  [body(): gathered = lax.all_to_all(spread, 'col', 0, 0, tiled=True)]
    unnamed x30 -> x24, local copies, waits for them, and re-layouts: 9.76 us -> 6.81 us
    pallas_call x5 -> x8, Pallas kernels: 10.9 us -> 13.6 us  [call(): pl.pallas_call(kernel, out_shape=tuple((jax.ShapeDtypeStruct(shape, dtype...]
    all_to_all x2, starting transfers between devices: 14.2 us -> 15.9 us  [exchange(): lax.all_to_all(value, ('leaf', 'col'), 0, 0, axis_index_groups=groups, ti...]
  transfers between devices with their start and end apart: 15 -> 15, of which waited for: 8 -> 9; matrix products, arithmetic and copies ran while one was open for 1% -> 0% of each run, Pallas kernels for 4% -> 9%
where the time goes in v3:
time: 137 us
  waiting for transfers between devices  60.9 us (44%)
  starting transfers between devices  40.3 us (29%)
  blocking collectives  14.8 us (11%)
  Pallas kernels  13.6 us (10%)
  local copies, waits for them, and re-layouts  6.81 us (5%)
    ppermute x12, waiting for transfers between devices, move(): return lax.ppermute(shard, 'col', pairs)  47 us
    ppermute x12, starting transfers between devices, move(): return lax.ppermute(shard, 'col', pairs)  20.9 us
    all_to_all x2, starting transfers between devices, exchange(): lax.all_to_all(value, ('leaf', 'col'), 0, 0, axis_index_groups=groups, ti...  15.9 us
    all_to_all x1, blocking collectives, exchange(): lax.all_to_all(value, ('leaf', 'col'), 0, 0, axis_index_groups=groups, ti...  14.8 us
    pallas_call x8, Pallas kernels, call(): pl.pallas_call(kernel, out_shape=tuple((jax.ShapeDtypeStruct(shape, dtype...  13.6 us
    all_to_all x2, waiting for transfers between devices, exchange(): lax.all_to_all(value, ('leaf', 'col'), 0, 0, axis_index_groups=groups, ti...  10.8 us
    unnamed x24, local copies, waits for them, and re-layouts  6.81 us
    all_to_all x1, starting transfers between devices, body(): gathered = lax.all_to_all(spread, 'col', 0, 0, tiled=True)  3.47 us
  transfers between devices with their start and end apart: 15, of which 9 were waited for; matrix products, arithmetic and copies ran while one was open for 0% of the time, Pallas kernels for 9%

profile of v3, /device:TPU:6, one launch (start us, length us, event | category | flops | bytes accessed | tf_op | source)
XLA Modules:
  0.0 136.6 jit_solution(7793577741193435206)
XLA Ops:
  0.0 3.5 %collective-permute-start = (f32[2,256,256]{2,1,0:T(8,128)}, f32[2,256,256]{2,1,0:T(8,128)S(1)}, u32[]{:S(2)}, u32[]{:S(2)}) collective-permute-start(f32[2,256,256]{2,1,0:T(8,128)} %own.3), channel_id=1, source_target_pairs={{0,1},{3,2},{4,5},{7,6},{8,9},{11,10},{12,13},{15,14},{16,17},{19,... | collective-permute-start | bytes 1572872 | tf_op jit(solution)/shard_map/ppermute | solution.py:180
  4.2 1.3 collective-permute-start.2
  5.5 9.4 %collective-permute-done.inner0 = f32[2,256,256]{2,1,0:T(8,128)S(1)} collective-permute-done((f32[2,256,256]{2,1,0:T(8,128)}, f32[2,256,256]{2,1,0:T(8,128)S(1)}, u32[]{:S(2)}, u32[]{:S(2)}) %collective-permute-start) | collective-permute-done | bytes 524320 | tf_op jit(solution)/shard_map/ppermute | solution.py:180
  15.0 4.7 %collective-permute-done.2.end0 = f32[2,256,256]{2,1,0:T(8,128)S(1)} collective-permute-done((f32[2,256,256]{2,1,0:T(8,128)}, f32[2,256,256]{2,1,0:T(8,128)S(1)}, u32[]{:S(2)}, u32[]{:S(2)}) %collective-permute-start.2) | collective-permute-done | bytes 524320 | tf_op jit(solution)/shard_map/ppermute | solution.py:180
  20.4 1.3 collective-permute-start.5
  21.7 5.4 %collective-permute-start.3 = (f32[2,256,256]{2,1,0:T(8,128)}, f32[2,256,256]{2,1,0:T(8,128)}, u32[]{:S(2)}, u32[]{:S(2)}) collective-permute-start(f32[2,256,256]{2,1,0:T(8,128)} %own.2), channel_id=1, source_target_pairs={{0,1},{3,2},{4,5},{7,6},{8,9},{11,10},{12,13},{15,14},{16,17},{19,... | collective-permute-start | bytes 1572872 | tf_op jit(solution)/shard_map/ppermute | solution.py:180
  27.1 7.7 %collective-permute-done.5.end1 = f32[2,256,256]{2,1,0:T(8,128)S(1)} collective-permute-done((f32[2,256,256]{2,1,0:T(8,128)S(1)}, f32[2,256,256]{2,1,0:T(8,128)S(1)}, u32[]{:S(2)}, u32[]{:S(2)}) %collective-permute-start.5) | collective-permute-done | bytes 524320 | tf_op jit(solution)/shard_map/ppermute | solution.py:180
  34.8 1.4 %collective-permute-start.7 = (f32[2,256,256]{2,1,0:T(8,128)}, f32[2,256,256]{2,1,0:T(8,128)}, u32[]{:S(2)}, u32[]{:S(2)}) collective-permute-start(f32[2,256,256]{2,1,0:T(8,128)} %own.2), channel_id=1, source_target_pairs={{1,2},{2,1},{5,6},{6,5},{9,10},{10,9},{13,14},{14,13},{17,18},{18,... | collective-permute-start | bytes 1572872 | tf_op jit(solution)/shard_map/ppermute | solution.py:180
  36.2 1.3 collective-permute-start.11
  37.5 1.5 %collective-permute-start.9 = (f32[2,256,256]{2,1,0:T(8,128)}, f32[2,256,256]{2,1,0:T(8,128)}, u32[]{:S(2)}, u32[]{:S(2)}) collective-permute-start(f32[2,256,256]{2,1,0:T(8,128)} %collective-permute-done.3.inner0), channel_id=1, source_target_pairs={{1,2},{2,1},{5,6},{6,5},{9,10},{10,9},{13,14},{14,13},{17,18},{18,... | collective-permute-start | bytes 1572872 | tf_op jit(solution)/shard_map/ppermute | solution.py:180
  39.0 1.3 collective-permute-start.6
  40.3 1.3 collective-permute-start.8
  41.6 1.6 %copy-done = f32[2,256,1024]{2,1,0:T(8,128)S(1)} copy-done((f32[2,256,1024]{2,1,0:T(8,128)S(1)}, f32[2,256,1024]{2,1,0:T(8,128)}, u32[]{:S(2)}) %copy-start) | copy-done | bytes 2097176
  43.2 1.0 copy-done.2
  44.2 1.0 near.3
  45.3 7.8 %collective-permute-done.11.end2 = f32[2,256,256]{2,1,0:T(8,128)} collective-permute-done((f32[2,256,256]{2,1,0:T(8,128)S(1)}, f32[2,256,256]{2,1,0:T(8,128)}, u32[]{:S(2)}, u32[]{:S(2)}) %collective-permute-start.11) | collective-permute-done | bytes 524320 | tf_op jit(solution)/shard_map/ppermute | solution.py:180
  53.1 2.0 %last.3 = (f32[2,256,256]{2,1,0:T(8,128)S(1)}, f32[2,256,256]{2,1,0:T(8,128)S(1)}) custom-call(f32[2,256,256]{2,1,0:T(8,128)S(1)} %get-tuple-element.32.part, bf16[2,256,256]{2,1,0:T(8,128)(2,1)S(1)} %get-tuple-element.33.far_high, bf16[2,256,256]{2,1,0:T(8,128)(2,1)S(1)} %get-tuple-element.34.far_low, f32[2,256,256]{2,1,0:T(8,128)S(1)} %collective-permute-done.4.across1, ...), custom_call_target="tpu_custom_call" | custom-call | flops 402653184 | bytes 4194304 | tf_op jit(solution)/shard_map/last/pallas_call | solution.py:48
  56.6 10.2 %all-to-all-start.1 = ((f32[8,64,256]{2,1,0:T(8,128)}), f32[8,64,256]{2,1,0:T(8,128)S(1)}, u32[]{:S(2)}, u32[]{:S(2)}) async-start(f32[8,64,256]{2,1,0:T(8,128)} %bitcast.5), calls=%async_computation.1 | async-start | bytes 1048576 | tf_op jit(solution)/shard_map/all_to_all | solution.py:201
  66.8 1.3 collective-permute-start.10
  68.1 13.0 %collective-permute-done.8.end1 = f32[2,256,256]{2,1,0:T(8,128)} collective-permute-done((f32[2,256,256]{2,1,0:T(8,128)}, f32[2,256,256]{2,1,0:T(8,128)}, u32[]{:S(2)}, u32[]{:S(2)}) %collective-permute-start.8) | collective-permute-done | bytes 524320 | tf_op jit(solution)/shard_map/ppermute | solution.py:180
  81.1 1.0 copy-done.7
  82.2 2.5 %near.2 = (f32[2,256,256]{2,1,0:T(8,128)S(1)}, bf16[2,256,256]{2,1,0:T(8,128)(2,1)S(1)}, bf16[2,256,256]{2,1,0:T(8,128)(2,1)S(1)}) custom-call(s32[1]{0:T(128)} %bitcast.place, f32[2,256,1024]{2,1,0:T(8,128)S(1)} %copy-done.1, f32[2,256,256]{2,1,0:T(8,128)S(1)} %copy-done.7, f32[2,256,256]{2,1,0:T(8,128)} %collective-permute-done.3.inner0, ...), custom_call_target="tpu_custom_call" | custom-call | flops 24159191040 | bytes 4194304 | tf_op jit(solution)/shard_map/near/pallas_call | solution.py:48
  86.2 1.2 all-to-all-done.1.pieces
  88.3 3.5 %all-to-all-start.2 = ((f32[4,2,64,256]{3,2,1,0:T(8,128)}), f32[4,2,64,256]{3,2,1,0:T(8,128)S(1)}, u32[]{:S(2)}, u32[]{:S(2)}) async-start(f32[4,2,64,256]{3,2,1,0:T(8,128)} %spread.1), calls=%async_computation.2 | async-start | bytes 1048576 | tf_op jit(solution)/shard_map/all_to_all | solution.py:242
  91.8 4.3 %collective-permute-done.10.end2 = f32[2,256,256]{2,1,0:T(8,128)} collective-permute-done((f32[2,256,256]{2,1,0:T(8,128)}, f32[2,256,256]{2,1,0:T(8,128)}, u32[]{:S(2)}, u32[]{:S(2)}) %collective-permute-start.10) | collective-permute-done | bytes 524320 | tf_op jit(solution)/shard_map/ppermute | solution.py:180
  96.1 2.9 %last.2 = (f32[2,256,256]{2,1,0:T(8,128)S(1)}, f32[2,256,256]{2,1,0:T(8,128)}) custom-call(f32[2,256,256]{2,1,0:T(8,128)S(1)} %copy-done.9, bf16[2,256,256]{2,1,0:T(8,128)(2,1)S(1)} %get-tuple-element.27.far_high, bf16[2,256,256]{2,1,0:T(8,128)(2,1)S(1)} %copy-done.11, f32[2,256,256]{2,1,0:T(8,128)} %collective-permute-done.9.across1, ...), custom_call_target="tpu_custom_call" | custom-call | flops 16106127360 | bytes 4194304 | tf_op jit(solution)/shard_map/last/pallas_call | solution.py:48
  99.0 3.0 %all-to-all-done.2.gathered = f32[4,2,64,256]{3,2,1,0:T(8,128)S(1)} async-done(((f32[4,2,64,256]{3,2,1,0:T(8,128)}), f32[4,2,64,256]{3,2,1,0:T(8,128)S(1)}, u32[]{:S(2)}, u32[]{:S(2)}) %all-to-all-start.2) | async-done | bytes 524320 | tf_op jit(solution)/shard_map/all_to_all | solution.py:242
  102.0 5.8 %all-to-all-start = ((f32[8,64,256]{2,1,0:T(8,128)}), f32[8,64,256]{2,1,0:T(8,128)S(1)}, u32[]{:S(2)}, u32[]{:S(2)}) async-start(f32[8,64,256]{2,1,0:T(8,128)} %bitcast.1), calls=%async_computation | async-start | bytes 1048576 | tf_op jit(solution)/shard_map/all_to_all | solution.py:201
  107.8 2.5 %invert.1.inverse = f32[256,256]{1,0:T(8,128)S(1)} custom-call(f32[4,2,64,256]{3,2,1,0:T(8,128)S(1)} %all-to-all-done.2.gathered), custom_call_target="tpu_custom_call" | custom-call | flops 1006632960 | bytes 4194304 | tf_op jit(solution)/shard_map/invert/pallas_call | solution.py:48
  110.3 9.6 %all-to-all-done.pieces = f32[8,64,256]{2,1,0:T(8,128)S(1)} async-done(((f32[8,64,256]{2,1,0:T(8,128)}), f32[8,64,256]{2,1,0:T(8,128)S(1)}, u32[]{:S(2)}, u32[]{:S(2)}) %all-to-all-start) | async-done | bytes 524320 | tf_op jit(solution)/shard_map/all_to_all | solution.py:201
  120.6 14.8 %all_to_all.20 = f32[8,64,256]{2,1,0:T(8,128)S(1)} all-to-all(f32[8,64,256]{2,1,0:T(8,128)S(1)} %coeffs.1), channel_id=1, replica_groups={{0,1,2,3,16,17,18,19},{4,5,6,7,20,21,22,23},{8,9,10,11,24,25,26,27},{12..., dimensions={0} | all-to-all | bytes 1048576 | tf_op jit(solution)/shard_map/all_to_all | solution.py:201
  135.4 1.2 final.1
  (31 shorter events, 6.0 us)
Async XLA Ops:
  0.0 15.0 %collective-permute-start = (f32[2,256,256]{2,1,0:T(8,128)}, f32[2,256,256]{2,1,0:T(8,128)S(1)}, u32[]{:S(2)}, u32[]{:S(2)}) collective-permute-start(f32[2,256,256]{2,1,0:T(8,128)} %own.3), channel_id=1, source_target_pairs={{0,1},{3,2},{4,5},{7,6},{8,9},{11,10},{12,13},{15,14},{16,17},{19,... | collective-permute-start | bytes 1572872 | tf_op jit(solution)/shard_map/ppermute | solution.py:180
  3.5 11.5 %collective-permute-start.1 = (f32[2,256,256]{2,1,0:T(8,128)}, f32[2,256,256]{2,1,0:T(8,128)S(1)}, u32[]{:S(2)}, u32[]{:S(2)}) collective-permute-start(f32[2,256,256]{2,1,0:T(8,128)} %own.3), channel_id=1, source_target_pairs={{1,2},{2,1},{5,6},{6,5},{9,10},{10,9},{13,14},{14,13},{17,18},{18,... | collective-permute-start | bytes 1572872 | tf_op jit(solution)/shard_map/ppermute | solution.py:180
  4.2 15.5 %collective-permute-start.2 = (f32[2,256,256]{2,1,0:T(8,128)}, f32[2,256,256]{2,1,0:T(8,128)S(1)}, u32[]{:S(2)}, u32[]{:S(2)}) collective-permute-start(f32[2,256,256]{2,1,0:T(8,128)} %own.3), channel_id=1, source_target_pairs={{1,0},{2,3},{5,4},{6,7},{9,8},{10,11},{13,12},{14,15},{17,16},{18,... | collective-permute-start | bytes 1572872 | tf_op jit(solution)/shard_map/ppermute | solution.py:180
  19.7 7.4 %collective-permute-start.4 = (f32[2,256,256]{2,1,0:T(8,128)S(1)}, f32[2,256,256]{2,1,0:T(8,128)S(1)}, u32[]{:S(2)}, u32[]{:S(2)}) collective-permute-start(f32[2,256,256]{2,1,0:T(8,128)S(1)} %collective-permute-done.inner0), channel_id=1, source_target_pairs={{1,2},{2,1},{5,6},{6,5},{9,10},{10,9},{13,14},{14,13},{17,18},{18,... | collective-permute-start | bytes 1572872 | tf_op jit(solution)/shard_map/ppermute | solution.py:180
  20.4 14.4 %collective-permute-start.5 = (f32[2,256,256]{2,1,0:T(8,128)S(1)}, f32[2,256,256]{2,1,0:T(8,128)S(1)}, u32[]{:S(2)}, u32[]{:S(2)}) collective-permute-start(f32[2,256,256]{2,1,0:T(8,128)S(1)} %collective-permute-done.1.across0), channel_id=1, source_target_pairs={{1,0},{2,3},{5,4},{6,7},{9,8},{10,11},{13,12},{14,15},{17,16},{18,... | collective-permute-start | bytes 1572872 | tf_op jit(solution)/shard_map/ppermute | solution.py:180
  21.7 15.8 %collective-permute-start.3 = (f32[2,256,256]{2,1,0:T(8,128)}, f32[2,256,256]{2,1,0:T(8,128)}, u32[]{:S(2)}, u32[]{:S(2)}) collective-permute-start(f32[2,256,256]{2,1,0:T(8,128)} %own.2), channel_id=1, source_target_pairs={{0,1},{3,2},{4,5},{7,6},{8,9},{11,10},{12,13},{15,14},{16,17},{19,... | collective-permute-start | bytes 1572872 | tf_op jit(solution)/shard_map/ppermute | solution.py:180
  34.8 5.5 %collective-permute-start.7 = (f32[2,256,256]{2,1,0:T(8,128)}, f32[2,256,256]{2,1,0:T(8,128)}, u32[]{:S(2)}, u32[]{:S(2)}) collective-permute-start(f32[2,256,256]{2,1,0:T(8,128)} %own.2), channel_id=1, source_target_pairs={{1,2},{2,1},{5,6},{6,5},{9,10},{10,9},{13,14},{14,13},{17,18},{18,... | collective-permute-start | bytes 1572872 | tf_op jit(solution)/shard_map/ppermute | solution.py:180
  36.2 16.8 %collective-permute-start.11 = (f32[2,256,256]{2,1,0:T(8,128)S(1)}, f32[2,256,256]{2,1,0:T(8,128)}, u32[]{:S(2)}, u32[]{:S(2)}) collective-permute-start(f32[2,256,256]{2,1,0:T(8,128)S(1)} %collective-permute-done.4.across1), channel_id=1, source_target_pairs={{1,0},{2,3},{5,4},{6,7},{9,8},{10,11},{13,12},{14,15},{17,16},{18,... | collective-permute-start | bytes 1572872 | tf_op jit(solution)/shard_map/ppermute | solution.py:180
  37.5 29.3 %collective-permute-start.9 = (f32[2,256,256]{2,1,0:T(8,128)}, f32[2,256,256]{2,1,0:T(8,128)}, u32[]{:S(2)}, u32[]{:S(2)}) collective-permute-start(f32[2,256,256]{2,1,0:T(8,128)} %collective-permute-done.3.inner0), channel_id=1, source_target_pairs={{1,2},{2,1},{5,6},{6,5},{9,10},{10,9},{13,14},{14,13},{17,18},{18,... | collective-permute-start | bytes 1572872 | tf_op jit(solution)/shard_map/ppermute | solution.py:180
  39.0 29.1 %collective-permute-start.6 = (f32[2,256,256]{2,1,0:T(8,128)}, f32[2,256,256]{2,1,0:T(8,128)}, u32[]{:S(2)}, u32[]{:S(2)}) collective-permute-start(f32[2,256,256]{2,1,0:T(8,128)} %own.2), channel_id=1, source_target_pairs={{1,0},{2,3},{5,4},{6,7},{9,8},{10,11},{13,12},{14,15},{17,16},{18,... | collective-permute-start | bytes 1572872 | tf_op jit(solution)/shard_map/ppermute | solution.py:180
  40.3 40.9 %collective-permute-start.8 = (f32[2,256,256]{2,1,0:T(8,128)}, f32[2,256,256]{2,1,0:T(8,128)}, u32[]{:S(2)}, u32[]{:S(2)}) collective-permute-start(f32[2,256,256]{2,1,0:T(8,128)} %collective-permute-done.7.across0), channel_id=1, source_target_pairs={{1,0},{2,3},{5,4},{6,7},{9,8},{10,11},{13,12},{14,15},{17,16},{18,... | collective-permute-start | bytes 1572872 | tf_op jit(solution)/shard_map/ppermute | solution.py:180
  41.6 1.6 %copy-start = (f32[2,256,1024]{2,1,0:T(8,128)S(1)}, f32[2,256,1024]{2,1,0:T(8,128)}, u32[]{:S(2)}) copy-start(f32[2,256,1024]{2,1,0:T(8,128)} %inverse.3) | copy-start | bytes 6291460
  43.2 1.0 copy-start.2
  44.2 8.9 %copy-start.3 = (f32[2,256,256]{2,1,0:T(8,128)S(1)}, f32[2,256,256]{2,1,0:T(8,128)}, u32[]{:S(2)}) copy-start(f32[2,256,256]{2,1,0:T(8,128)} %right.3) | copy-start | bytes 1572868
  45.2 35.9 %copy-start.1 = (f32[2,256,1024]{2,1,0:T(8,128)S(1)}, f32[2,256,1024]{2,1,0:T(8,128)}, u32[]{:S(2)}) copy-start(f32[2,256,1024]{2,1,0:T(8,128)} %inverse.3) | copy-start | bytes 6291460
  55.0 0.8 copy-start.5
  55.8 0.8 copy-start.4
  56.6 30.8 %all-to-all-start.1 = ((f32[8,64,256]{2,1,0:T(8,128)}), f32[8,64,256]{2,1,0:T(8,128)S(1)}, u32[]{:S(2)}, u32[]{:S(2)}) async-start(f32[8,64,256]{2,1,0:T(8,128)} %bitcast.5), calls=%async_computation.1 | async-start | bytes 1048576 | tf_op jit(solution)/shard_map/all_to_all | solution.py:201
  66.8 29.3 %collective-permute-start.10 = (f32[2,256,256]{2,1,0:T(8,128)}, f32[2,256,256]{2,1,0:T(8,128)}, u32[]{:S(2)}, u32[]{:S(2)}) collective-permute-start(f32[2,256,256]{2,1,0:T(8,128)} %collective-permute-done.9.across1), channel_id=1, source_target_pairs={{1,0},{2,3},{5,4},{6,7},{9,8},{10,11},{13,12},{14,15},{17,16},{18,... | collective-permute-start | bytes 1572872 | tf_op jit(solution)/shard_map/ppermute | solution.py:180
  81.1 1.0 copy-start.7
  84.7 0.8 copy-start.8
  85.5 0.7 copy-start.10
  87.5 8.6 %copy-start.9 = (f32[2,256,256]{2,1,0:T(8,128)S(1)}, f32[2,256,256]{2,1,0:T(8,128)}, u32[]{:S(2)}) copy-start(f32[2,256,256]{2,1,0:T(8,128)} %copy-done.8) | copy-start | bytes 1572868
  87.5 8.6 %copy-start.11 = (bf16[2,256,256]{2,1,0:T(8,128)(2,1)S(1)}, bf16[2,256,256]{2,1,0:T(8,128)(2,1)}, u32[]{:S(2)}) copy-start(bf16[2,256,256]{2,1,0:T(8,128)(2,1)} %copy-done.10) | copy-start | bytes 786436
  88.3 13.7 %all-to-all-start.2 = ((f32[4,2,64,256]{3,2,1,0:T(8,128)}), f32[4,2,64,256]{3,2,1,0:T(8,128)S(1)}, u32[]{:S(2)}, u32[]{:S(2)}) async-start(f32[4,2,64,256]{3,2,1,0:T(8,128)} %spread.1), calls=%async_computation.2 | async-start | bytes 1048576 | tf_op jit(solution)/shard_map/all_to_all | solution.py:242
  102.0 17.9 %all-to-all-start = ((f32[8,64,256]{2,1,0:T(8,128)}), f32[8,64,256]{2,1,0:T(8,128)S(1)}, u32[]{:S(2)}, u32[]{:S(2)}) async-start(f32[8,64,256]{2,1,0:T(8,128)} %bitcast.1), calls=%async_computation | async-start | bytes 1048576 | tf_op jit(solution)/shard_map/all_to_all | solution.py:201
  110.3 25.1 %copy-start.6 = (f32[2,256,256]{2,1,0:T(8,128)S(1)}, f32[2,256,256]{2,1,0:T(8,128)}, u32[]{:S(2)}) copy-start(f32[2,256,256]{2,1,0:T(8,128)} %copy-done.5) | copy-start | bytes 1572868

commit v4 on v3

--- a/solution.py
+++ b/solution.py
@@ -63,13 +63,18 @@
     return [pl.ds(pl.multiple_of(index * rows, rows), rows) for index in indices]
 
 
-def near_kernel(place, inverse, own, inner0, end0, across0, end1, part, far_high, far_low):
+def fourth_kernel(place, inverse, far_high, far_low):
+    strips = block_columns(place[0], inverse.shape[1])
+    for leaf in range(inverse.shape[0]):
+        far_high[leaf], far_low[leaf] = split(inverse[leaf, :, strips[3]])
+
+
+def near_kernel(place, inverse, own, inner0, end0, across0, end1, part):
     strips = block_columns(place[0], own.shape[1])
     for leaf in range(own.shape[0]):
         total = mul(inverse[leaf, :, strips[0]], own[leaf])
         total += mul(inverse[leaf, :, strips[1]], inner0[leaf] + end0[leaf])
         part[leaf] = total + mul(inverse[leaf, :, strips[2]], across0[leaf] + end1[leaf])
-        far_high[leaf], far_low[leaf] = split(inverse[leaf, :, strips[3]])
 
 
 def last_kernel(part, far_high, far_low, across1, end2, right, solved, small):
@@ -204,7 +209,7 @@
         return call(
             near_kernel,
             "near",
-            (both, strips, strips),
+            (both,),
             (place, leaf_inverse) + gens,
             weight * 6 * unit,
             scalars=1,
@@ -212,13 +217,16 @@
 
     def last(weight, parts, *gens):
         return call(
-            last_kernel, "last", (both, small), (*parts, *gens, right_gen), weight * 4 * unit
+            last_kernel, "last", (both, small), (*parts, *far, *gens, right_gen), weight * 4 * unit
         )
 
+    far = call(
+        fourth_kernel, "fourth", (strips, strips), (place, leaf_inverse), unit, scalars=1
+    )
     inner0 = move(left_gen, TO_INNER)
     across0 = move(left_gen, ACROSS)
     end0 = move(left_gen, TO_END)
-    inner0, across0, end0, parent = lax.optimization_barrier((inner0, across0, end0, parent_gen))
+    across0, inner0, end0, parent = lax.optimization_barrier((across0, inner0, end0, parent_gen))
     across1 = move(inner0, ACROSS)
     end1 = move(across0, TO_END)
     inner0_p = move(parent, TO_INNER)

time: 137 us -> 137 us (level)
    pallas_call x8 -> x9, Pallas kernels: 13.6 us -> 13.5 us  [call(): pl.pallas_call(kernel, out_shape=tuple((jax.ShapeDtypeStruct(shape, dtype...]
where the time goes in v4:
time: 137 us
  waiting for transfers between devices  61.8 us (45%)
  starting transfers between devices  40.3 us (29%)
  blocking collectives  14.8 us (11%)
  Pallas kernels  13.5 us (10%)
  local copies, waits for them, and re-layouts  6 us (4%)
    ppermute x12, waiting for transfers between devices, move(): return lax.ppermute(shard, 'col', pairs)  47.1 us
    ppermute x12, starting transfers between devices, move(): return lax.ppermute(shard, 'col', pairs)  20.9 us
    all_to_all x2, starting transfers between devices, exchange(): lax.all_to_all(value, ('leaf', 'col'), 0, 0, axis_index_groups=groups, ti...  15.9 us
    all_to_all x1, blocking collectives, exchange(): lax.all_to_all(value, ('leaf', 'col'), 0, 0, axis_index_groups=groups, ti...  14.8 us
    pallas_call x9, Pallas kernels, call(): pl.pallas_call(kernel, out_shape=tuple((jax.ShapeDtypeStruct(shape, dtype...  13.5 us
    all_to_all x2, waiting for transfers between devices, exchange(): lax.all_to_all(value, ('leaf', 'col'), 0, 0, axis_index_groups=groups, ti...  11.7 us
    unnamed x24, local copies, waits for them, and re-layouts  6 us
    all_to_all x1, starting transfers between devices, body(): gathered = lax.all_to_all(spread, 'col', 0, 0, tiled=True)  3.47 us
  transfers between devices with their start and end apart: 15, of which 9 were waited for; matrix products, arithmetic and copies ran while one was open for 0% of the time, Pallas kernels for 9%

profile of v4, /device:TPU:6, one launch (start us, length us, event | category | flops | bytes accessed | tf_op | source)
XLA Modules:
  0.0 136.6 jit_solution(13567099004599678224)
XLA Ops:
  0.0 3.5 %collective-permute-start.1 = (f32[2,256,256]{2,1,0:T(8,128)}, f32[2,256,256]{2,1,0:T(8,128)S(1)}, u32[]{:S(2)}, u32[]{:S(2)}) collective-permute-start(f32[2,256,256]{2,1,0:T(8,128)} %own.3), channel_id=1, source_target_pairs={{0,1},{3,2},{4,5},{7,6},{8,9},{11,10},{12,13},{15,14},{16,17},{19,... | collective-permute-start | bytes 1572872 | tf_op jit(solution)/shard_map/ppermute | solution.py:185
  4.2 1.3 collective-permute-start.2
  5.5 9.4 %collective-permute-done.1.inner0 = f32[2,256,256]{2,1,0:T(8,128)S(1)} collective-permute-done((f32[2,256,256]{2,1,0:T(8,128)}, f32[2,256,256]{2,1,0:T(8,128)S(1)}, u32[]{:S(2)}, u32[]{:S(2)}) %collective-permute-start.1) | collective-permute-done | bytes 524320 | tf_op jit(solution)/shard_map/ppermute | solution.py:185
  15.0 4.7 %collective-permute-done.2.end0 = f32[2,256,256]{2,1,0:T(8,128)S(1)} collective-permute-done((f32[2,256,256]{2,1,0:T(8,128)}, f32[2,256,256]{2,1,0:T(8,128)S(1)}, u32[]{:S(2)}, u32[]{:S(2)}) %collective-permute-start.2) | collective-permute-done | bytes 524320 | tf_op jit(solution)/shard_map/ppermute | solution.py:185
  20.4 1.3 collective-permute-start.5
  21.7 5.4 %collective-permute-start.3 = (f32[2,256,256]{2,1,0:T(8,128)}, f32[2,256,256]{2,1,0:T(8,128)}, u32[]{:S(2)}, u32[]{:S(2)}) collective-permute-start(f32[2,256,256]{2,1,0:T(8,128)} %own.2), channel_id=1, source_target_pairs={{0,1},{3,2},{4,5},{7,6},{8,9},{11,10},{12,13},{15,14},{16,17},{19,... | collective-permute-start | bytes 1572872 | tf_op jit(solution)/shard_map/ppermute | solution.py:185
  27.1 7.7 %collective-permute-done.5.end1 = f32[2,256,256]{2,1,0:T(8,128)S(1)} collective-permute-done((f32[2,256,256]{2,1,0:T(8,128)S(1)}, f32[2,256,256]{2,1,0:T(8,128)S(1)}, u32[]{:S(2)}, u32[]{:S(2)}) %collective-permute-start.5) | collective-permute-done | bytes 524320 | tf_op jit(solution)/shard_map/ppermute | solution.py:185
  34.8 1.5 %collective-permute-start.7 = (f32[2,256,256]{2,1,0:T(8,128)}, f32[2,256,256]{2,1,0:T(8,128)}, u32[]{:S(2)}, u32[]{:S(2)}) collective-permute-start(f32[2,256,256]{2,1,0:T(8,128)} %own.2), channel_id=1, source_target_pairs={{1,2},{2,1},{5,6},{6,5},{9,10},{10,9},{13,14},{14,13},{17,18},{18,... | collective-permute-start | bytes 1572872 | tf_op jit(solution)/shard_map/ppermute | solution.py:185
  36.2 1.3 collective-permute-start.11
  37.5 1.5 %collective-permute-start.9 = (f32[2,256,256]{2,1,0:T(8,128)}, f32[2,256,256]{2,1,0:T(8,128)}, u32[]{:S(2)}, u32[]{:S(2)}) collective-permute-start(f32[2,256,256]{2,1,0:T(8,128)} %collective-permute-done.3.inner0), channel_id=1, source_target_pairs={{1,2},{2,1},{5,6},{6,5},{9,10},{10,9},{13,14},{14,13},{17,18},{18,... | collective-permute-start | bytes 1572872 | tf_op jit(solution)/shard_map/ppermute | solution.py:185
  39.0 1.3 collective-permute-start.6
  40.3 1.3 collective-permute-start.8
  41.6 1.6 %copy-done = f32[2,256,1024]{2,1,0:T(8,128)S(1)} copy-done((f32[2,256,1024]{2,1,0:T(8,128)S(1)}, f32[2,256,1024]{2,1,0:T(8,128)}, u32[]{:S(2)}) %copy-start) | copy-done | bytes 2097176
  43.3 1.0 copy-done.6
  44.2 0.9 near.3.part
  45.2 7.9 %collective-permute-done.11.end2 = f32[2,256,256]{2,1,0:T(8,128)} collective-permute-done((f32[2,256,256]{2,1,0:T(8,128)S(1)}, f32[2,256,256]{2,1,0:T(8,128)}, u32[]{:S(2)}, u32[]{:S(2)}) %collective-permute-start.11) | collective-permute-done | bytes 524320 | tf_op jit(solution)/shard_map/ppermute | solution.py:185
  53.1 2.0 %last.3 = (f32[2,256,256]{2,1,0:T(8,128)S(1)}, f32[2,256,256]{2,1,0:T(8,128)S(1)}) custom-call(f32[2,256,256]{2,1,0:T(8,128)S(1)} %near.3.part, bf16[2,256,256]{2,1,0:T(8,128)(2,1)S(1)} %get-tuple-element.22.far_high, bf16[2,256,256]{2,1,0:T(8,128)(2,1)S(1)} %get-tuple-element.23.far_low, f32[2,256,256]{2,1,0:T(8,128)S(1)} %collective-permute-done.4.across1, ...), custom_call_target="tpu_custom_call" | custom-call | flops 402653184 | bytes 4194304 | tf_op jit(solution)/shard_map/last/pallas_call | solution.py:48
  56.6 10.2 %all-to-all-start.1 = ((f32[8,64,256]{2,1,0:T(8,128)}), f32[8,64,256]{2,1,0:T(8,128)S(1)}, u32[]{:S(2)}, u32[]{:S(2)}) async-start(f32[8,64,256]{2,1,0:T(8,128)} %bitcast.5), calls=%async_computation.1 | async-start | bytes 1048576 | tf_op jit(solution)/shard_map/all_to_all | solution.py:206
  66.8 1.3 collective-permute-start.10
  68.1 13.0 %collective-permute-done.8.end1 = f32[2,256,256]{2,1,0:T(8,128)} collective-permute-done((f32[2,256,256]{2,1,0:T(8,128)}, f32[2,256,256]{2,1,0:T(8,128)}, u32[]{:S(2)}, u32[]{:S(2)}) %collective-permute-start.8) | collective-permute-done | bytes 524320 | tf_op jit(solution)/shard_map/ppermute | solution.py:185
  81.2 1.0 copy-done.9
  82.2 2.4 %near.2.part = f32[2,256,256]{2,1,0:T(8,128)S(1)} custom-call(s32[1]{0:T(128)} %bitcast.place, f32[2,256,1024]{2,1,0:T(8,128)S(1)} %copy-done.1, f32[2,256,256]{2,1,0:T(8,128)S(1)} %copy-done.9, f32[2,256,256]{2,1,0:T(8,128)} %collective-permute-done.3.inner0, f32[2,256,256]{2,1,0:T(8,128)} %collective-permute-done.6.end0, ...), custom_call_target="tpu_custom_call" | custom-call | flops 24159191040 | bytes 4194304 | tf_op jit(solution)/shard_map/near/pallas_call | solution.py:48
  85.4 2.1 %all-to-all-done.1.pieces = f32[8,64,256]{2,1,0:T(8,128)S(1)} async-done(((f32[8,64,256]{2,1,0:T(8,128)}), f32[8,64,256]{2,1,0:T(8,128)S(1)}, u32[]{:S(2)}, u32[]{:S(2)}) %all-to-all-start.1) | async-done | bytes 524320 | tf_op jit(solution)/shard_map/all_to_all | solution.py:206
  88.3 3.5 %all-to-all-start.2 = ((f32[4,2,64,256]{3,2,1,0:T(8,128)}), f32[4,2,64,256]{3,2,1,0:T(8,128)S(1)}, u32[]{:S(2)}, u32[]{:S(2)}) async-start(f32[4,2,64,256]{3,2,1,0:T(8,128)} %spread.1), calls=%async_computation.2 | async-start | bytes 1048576 | tf_op jit(solution)/shard_map/all_to_all | solution.py:250
  91.8 4.3 %collective-permute-done.10.end2 = f32[2,256,256]{2,1,0:T(8,128)} collective-permute-done((f32[2,256,256]{2,1,0:T(8,128)}, f32[2,256,256]{2,1,0:T(8,128)}, u32[]{:S(2)}, u32[]{:S(2)}) %collective-permute-start.10) | collective-permute-done | bytes 524320 | tf_op jit(solution)/shard_map/ppermute | solution.py:185
  96.1 2.9 %last.2 = (f32[2,256,256]{2,1,0:T(8,128)S(1)}, f32[2,256,256]{2,1,0:T(8,128)}) custom-call(f32[2,256,256]{2,1,0:T(8,128)S(1)} %copy-done.11, bf16[2,256,256]{2,1,0:T(8,128)(2,1)S(1)} %get-tuple-element.22.far_high, bf16[2,256,256]{2,1,0:T(8,128)(2,1)S(1)} %copy-done.8, f32[2,256,256]{2,1,0:T(8,128)} %collective-permute-done.9.across1, ...), custom_call_target="tpu_custom_call" | custom-call | flops 16106127360 | bytes 4194304 | tf_op jit(solution)/shard_map/last/pallas_call | solution.py:48
  99.0 3.0 %all-to-all-done.2.gathered = f32[4,2,64,256]{3,2,1,0:T(8,128)S(1)} async-done(((f32[4,2,64,256]{3,2,1,0:T(8,128)}), f32[4,2,64,256]{3,2,1,0:T(8,128)S(1)}, u32[]{:S(2)}, u32[]{:S(2)}) %all-to-all-start.2) | async-done | bytes 524320 | tf_op jit(solution)/shard_map/all_to_all | solution.py:250
  102.0 5.7 %all-to-all-start = ((f32[8,64,256]{2,1,0:T(8,128)}), f32[8,64,256]{2,1,0:T(8,128)S(1)}, u32[]{:S(2)}, u32[]{:S(2)}) async-start(f32[8,64,256]{2,1,0:T(8,128)} %bitcast.1), calls=%async_computation | async-start | bytes 1048576 | tf_op jit(solution)/shard_map/all_to_all | solution.py:206
  107.8 2.5 %invert.1.inverse = f32[256,256]{1,0:T(8,128)S(1)} custom-call(f32[4,2,64,256]{3,2,1,0:T(8,128)S(1)} %all-to-all-done.2.gathered), custom_call_target="tpu_custom_call" | custom-call | flops 1006632960 | bytes 4194304 | tf_op jit(solution)/shard_map/invert/pallas_call | solution.py:48
  110.4 9.6 %all-to-all-done.pieces = f32[8,64,256]{2,1,0:T(8,128)S(1)} async-done(((f32[8,64,256]{2,1,0:T(8,128)}), f32[8,64,256]{2,1,0:T(8,128)S(1)}, u32[]{:S(2)}, u32[]{:S(2)}) %all-to-all-start) | async-done | bytes 524320 | tf_op jit(solution)/shard_map/all_to_all | solution.py:206
  120.6 14.8 %all_to_all.20 = f32[8,64,256]{2,1,0:T(8,128)S(1)} all-to-all(f32[8,64,256]{2,1,0:T(8,128)S(1)} %coeffs.1), channel_id=1, replica_groups={{0,1,2,3,16,17,18,19},{4,5,6,7,20,21,22,23},{8,9,10,11,24,25,26,27},{12..., dimensions={0} | all-to-all | bytes 1048576 | tf_op jit(solution)/shard_map/all_to_all | solution.py:206
  135.4 1.2 final.1
  (32 shorter events, 5.3 us)
Async XLA Ops:
  0.0 15.0 %collective-permute-start.1 = (f32[2,256,256]{2,1,0:T(8,128)}, f32[2,256,256]{2,1,0:T(8,128)S(1)}, u32[]{:S(2)}, u32[]{:S(2)}) collective-permute-start(f32[2,256,256]{2,1,0:T(8,128)} %own.3), channel_id=1, source_target_pairs={{0,1},{3,2},{4,5},{7,6},{8,9},{11,10},{12,13},{15,14},{16,17},{19,... | collective-permute-start | bytes 1572872 | tf_op jit(solution)/shard_map/ppermute | solution.py:185
  3.5 11.5 %collective-permute-start = (f32[2,256,256]{2,1,0:T(8,128)}, f32[2,256,256]{2,1,0:T(8,128)S(1)}, u32[]{:S(2)}, u32[]{:S(2)}) collective-permute-start(f32[2,256,256]{2,1,0:T(8,128)} %own.3), channel_id=1, source_target_pairs={{1,2},{2,1},{5,6},{6,5},{9,10},{10,9},{13,14},{14,13},{17,18},{18,... | collective-permute-start | bytes 1572872 | tf_op jit(solution)/shard_map/ppermute | solution.py:185
  4.2 15.5 %collective-permute-start.2 = (f32[2,256,256]{2,1,0:T(8,128)}, f32[2,256,256]{2,1,0:T(8,128)S(1)}, u32[]{:S(2)}, u32[]{:S(2)}) collective-permute-start(f32[2,256,256]{2,1,0:T(8,128)} %own.3), channel_id=1, source_target_pairs={{1,0},{2,3},{5,4},{6,7},{9,8},{10,11},{13,12},{14,15},{17,16},{18,... | collective-permute-start | bytes 1572872 | tf_op jit(solution)/shard_map/ppermute | solution.py:185
  19.7 7.4 %collective-permute-start.4 = (f32[2,256,256]{2,1,0:T(8,128)S(1)}, f32[2,256,256]{2,1,0:T(8,128)S(1)}, u32[]{:S(2)}, u32[]{:S(2)}) collective-permute-start(f32[2,256,256]{2,1,0:T(8,128)S(1)} %collective-permute-done.1.inner0), channel_id=1, source_target_pairs={{1,2},{2,1},{5,6},{6,5},{9,10},{10,9},{13,14},{14,13},{17,18},{18,... | collective-permute-start | bytes 1572872 | tf_op jit(solution)/shard_map/ppermute | solution.py:185
  20.4 14.4 %collective-permute-start.5 = (f32[2,256,256]{2,1,0:T(8,128)S(1)}, f32[2,256,256]{2,1,0:T(8,128)S(1)}, u32[]{:S(2)}, u32[]{:S(2)}) collective-permute-start(f32[2,256,256]{2,1,0:T(8,128)S(1)} %collective-permute-done.across0), channel_id=1, source_target_pairs={{1,0},{2,3},{5,4},{6,7},{9,8},{10,11},{13,12},{14,15},{17,16},{18,... | collective-permute-start | bytes 1572872 | tf_op jit(solution)/shard_map/ppermute | solution.py:185
  21.7 15.8 %collective-permute-start.3 = (f32[2,256,256]{2,1,0:T(8,128)}, f32[2,256,256]{2,1,0:T(8,128)}, u32[]{:S(2)}, u32[]{:S(2)}) collective-permute-start(f32[2,256,256]{2,1,0:T(8,128)} %own.2), channel_id=1, source_target_pairs={{0,1},{3,2},{4,5},{7,6},{8,9},{11,10},{12,13},{15,14},{16,17},{19,... | collective-permute-start | bytes 1572872 | tf_op jit(solution)/shard_map/ppermute | solution.py:185
  34.8 5.5 %collective-permute-start.7 = (f32[2,256,256]{2,1,0:T(8,128)}, f32[2,256,256]{2,1,0:T(8,128)}, u32[]{:S(2)}, u32[]{:S(2)}) collective-permute-start(f32[2,256,256]{2,1,0:T(8,128)} %own.2), channel_id=1, source_target_pairs={{1,2},{2,1},{5,6},{6,5},{9,10},{10,9},{13,14},{14,13},{17,18},{18,... | collective-permute-start | bytes 1572872 | tf_op jit(solution)/shard_map/ppermute | solution.py:185
  36.2 16.8 %collective-permute-start.11 = (f32[2,256,256]{2,1,0:T(8,128)S(1)}, f32[2,256,256]{2,1,0:T(8,128)}, u32[]{:S(2)}, u32[]{:S(2)}) collective-permute-start(f32[2,256,256]{2,1,0:T(8,128)S(1)} %collective-permute-done.4.across1), channel_id=1, source_target_pairs={{1,0},{2,3},{5,4},{6,7},{9,8},{10,11},{13,12},{14,15},{17,16},{18,... | collective-permute-start | bytes 1572872 | tf_op jit(solution)/shard_map/ppermute | solution.py:185
  37.5 29.3 %collective-permute-start.9 = (f32[2,256,256]{2,1,0:T(8,128)}, f32[2,256,256]{2,1,0:T(8,128)}, u32[]{:S(2)}, u32[]{:S(2)}) collective-permute-start(f32[2,256,256]{2,1,0:T(8,128)} %collective-permute-done.3.inner0), channel_id=1, source_target_pairs={{1,2},{2,1},{5,6},{6,5},{9,10},{10,9},{13,14},{14,13},{17,18},{18,... | collective-permute-start | bytes 1572872 | tf_op jit(solution)/shard_map/ppermute | solution.py:185
  39.0 29.1 %collective-permute-start.6 = (f32[2,256,256]{2,1,0:T(8,128)}, f32[2,256,256]{2,1,0:T(8,128)}, u32[]{:S(2)}, u32[]{:S(2)}) collective-permute-start(f32[2,256,256]{2,1,0:T(8,128)} %own.2), channel_id=1, source_target_pairs={{1,0},{2,3},{5,4},{6,7},{9,8},{10,11},{13,12},{14,15},{17,16},{18,... | collective-permute-start | bytes 1572872 | tf_op jit(solution)/shard_map/ppermute | solution.py:185
  40.3 40.9 %collective-permute-start.8 = (f32[2,256,256]{2,1,0:T(8,128)}, f32[2,256,256]{2,1,0:T(8,128)}, u32[]{:S(2)}, u32[]{:S(2)}) collective-permute-start(f32[2,256,256]{2,1,0:T(8,128)} %collective-permute-done.7.across0), channel_id=1, source_target_pairs={{1,0},{2,3},{5,4},{6,7},{9,8},{10,11},{13,12},{14,15},{17,16},{18,... | collective-permute-start | bytes 1572872 | tf_op jit(solution)/shard_map/ppermute | solution.py:185
  41.6 1.6 %copy-start = (f32[2,256,1024]{2,1,0:T(8,128)S(1)}, f32[2,256,1024]{2,1,0:T(8,128)}, u32[]{:S(2)}) copy-start(f32[2,256,1024]{2,1,0:T(8,128)} %inverse.5) | copy-start | bytes 6291460
  43.2 1.0 copy-start.6
  44.2 8.8 %copy-start.7 = (bf16[2,256,256]{2,1,0:T(8,128)(2,1)}, bf16[2,256,256]{2,1,0:T(8,128)(2,1)S(1)}, u32[]{:S(2)}) copy-start(bf16[2,256,256]{2,1,0:T(8,128)(2,1)S(1)} %get-tuple-element.23.far_low) | copy-start | bytes 786436
  44.2 8.8 %copy-start.2 = (f32[2,256,256]{2,1,0:T(8,128)S(1)}, f32[2,256,256]{2,1,0:T(8,128)}, u32[]{:S(2)}) copy-start(f32[2,256,256]{2,1,0:T(8,128)} %right.3) | copy-start | bytes 1572868
  45.1 36.0 %copy-start.1 = (f32[2,256,1024]{2,1,0:T(8,128)S(1)}, f32[2,256,1024]{2,1,0:T(8,128)}, u32[]{:S(2)}) copy-start(f32[2,256,1024]{2,1,0:T(8,128)} %inverse.5) | copy-start | bytes 6291460
  55.0 0.8 copy-start.3
  55.8 0.8 copy-start.4
  56.6 30.8 %all-to-all-start.1 = ((f32[8,64,256]{2,1,0:T(8,128)}), f32[8,64,256]{2,1,0:T(8,128)S(1)}, u32[]{:S(2)}, u32[]{:S(2)}) async-start(f32[8,64,256]{2,1,0:T(8,128)} %bitcast.5), calls=%async_computation.1 | async-start | bytes 1048576 | tf_op jit(solution)/shard_map/all_to_all | solution.py:206
  66.8 29.3 %collective-permute-start.10 = (f32[2,256,256]{2,1,0:T(8,128)}, f32[2,256,256]{2,1,0:T(8,128)}, u32[]{:S(2)}, u32[]{:S(2)}) collective-permute-start(f32[2,256,256]{2,1,0:T(8,128)} %collective-permute-done.9.across1), channel_id=1, source_target_pairs={{1,0},{2,3},{5,4},{6,7},{9,8},{10,11},{13,12},{14,15},{17,16},{18,... | collective-permute-start | bytes 1572872 | tf_op jit(solution)/shard_map/ppermute | solution.py:185
  81.2 1.0 copy-start.9
  84.6 0.8 copy-start.10
  85.4 10.7 %copy-start.8 = (bf16[2,256,256]{2,1,0:T(8,128)(2,1)S(1)}, bf16[2,256,256]{2,1,0:T(8,128)(2,1)}, u32[]{:S(2)}) copy-start(bf16[2,256,256]{2,1,0:T(8,128)(2,1)} %copy-done.7) | copy-start | bytes 786436
  87.5 8.6 %copy-start.11 = (f32[2,256,256]{2,1,0:T(8,128)S(1)}, f32[2,256,256]{2,1,0:T(8,128)}, u32[]{:S(2)}) copy-start(f32[2,256,256]{2,1,0:T(8,128)} %copy-done.10) | copy-start | bytes 1572868
  88.3 13.7 %all-to-all-start.2 = ((f32[4,2,64,256]{3,2,1,0:T(8,128)}), f32[4,2,64,256]{3,2,1,0:T(8,128)S(1)}, u32[]{:S(2)}, u32[]{:S(2)}) async-start(f32[4,2,64,256]{3,2,1,0:T(8,128)} %spread.1), calls=%async_computation.2 | async-start | bytes 1048576 | tf_op jit(solution)/shard_map/all_to_all | solution.py:250
  102.0 17.9 %all-to-all-start = ((f32[8,64,256]{2,1,0:T(8,128)}), f32[8,64,256]{2,1,0:T(8,128)S(1)}, u32[]{:S(2)}, u32[]{:S(2)}) async-start(f32[8,64,256]{2,1,0:T(8,128)} %bitcast.1), calls=%async_computation | async-start | bytes 1048576 | tf_op jit(solution)/shard_map/all_to_all | solution.py:206
  110.3 25.1 %copy-start.5 = (f32[2,256,256]{2,1,0:T(8,128)S(1)}, f32[2,256,256]{2,1,0:T(8,128)}, u32[]{:S(2)}) copy-start(f32[2,256,256]{2,1,0:T(8,128)} %copy-done.4) | copy-start | bytes 1572868

commit v5 on v3

--- a/solution.py
+++ b/solution.py
@@ -12,7 +12,7 @@
 NN = (((1,), (0,)), ((), ()))
 NT = (((1,), (1,)), ((), ()))
 TN = (((0,), (0,)), ((), ()))
-PARAMS = pltpu.CompilerParams(vmem_limit_bytes=16 * 1024 * 1024)
+PARAMS = pltpu.CompilerParams(vmem_limit_bytes=8 * 1024 * 1024)
 SETTLED = 2.4e-4
 DOUBLINGS = 9
 WEIGHT = 40

time: 137 us -> 137 us (level)
  no operation moved by 1% of the time
where the time goes in v5:
time: 137 us
  waiting for transfers between devices  60.9 us (44%)
  starting transfers between devices  40.3 us (29%)
  blocking collectives  14.8 us (11%)
  Pallas kernels  13.6 us (10%)
  local copies, waits for them, and re-layouts  6.81 us (5%)
    ppermute x12, waiting for transfers between devices, move(): return lax.ppermute(shard, 'col', pairs)  47 us
    ppermute x12, starting transfers between devices, move(): return lax.ppermute(shard, 'col', pairs)  20.9 us
    all_to_all x2, starting transfers between devices, exchange(): lax.all_to_all(value, ('leaf', 'col'), 0, 0, axis_index_groups=groups, ti...  15.9 us
    all_to_all x1, blocking collectives, exchange(): lax.all_to_all(value, ('leaf', 'col'), 0, 0, axis_index_groups=groups, ti...  14.8 us
    pallas_call x8, Pallas kernels, call(): pl.pallas_call(kernel, out_shape=tuple((jax.ShapeDtypeStruct(shape, dtype...  13.6 us
    all_to_all x2, waiting for transfers between devices, exchange(): lax.all_to_all(value, ('leaf', 'col'), 0, 0, axis_index_groups=groups, ti...  10.8 us
    unnamed x24, local copies, waits for them, and re-layouts  6.81 us
    all_to_all x1, starting transfers between devices, body(): gathered = lax.all_to_all(spread, 'col', 0, 0, tiled=True)  3.47 us
  transfers between devices with their start and end apart: 15, of which 9 were waited for; matrix products, arithmetic and copies ran while one was open for 0% of the time, Pallas kernels for 9%

profile of v5, /device:TPU:6, one launch (start us, length us, event | category | flops | bytes accessed | tf_op | source)
XLA Modules:
  0.0 136.6 jit_solution(8781006176539331680)
XLA Ops:
  0.0 3.5 %collective-permute-start = (f32[2,256,256]{2,1,0:T(8,128)}, f32[2,256,256]{2,1,0:T(8,128)S(1)}, u32[]{:S(2)}, u32[]{:S(2)}) collective-permute-start(f32[2,256,256]{2,1,0:T(8,128)} %own.3), channel_id=1, source_target_pairs={{0,1},{3,2},{4,5},{7,6},{8,9},{11,10},{12,13},{15,14},{16,17},{19,... | collective-permute-start | bytes 1572872 | tf_op jit(solution)/shard_map/ppermute | solution.py:180
  4.2 1.3 collective-permute-start.2
  5.5 9.4 %collective-permute-done.inner0 = f32[2,256,256]{2,1,0:T(8,128)S(1)} collective-permute-done((f32[2,256,256]{2,1,0:T(8,128)}, f32[2,256,256]{2,1,0:T(8,128)S(1)}, u32[]{:S(2)}, u32[]{:S(2)}) %collective-permute-start) | collective-permute-done | bytes 524320 | tf_op jit(solution)/shard_map/ppermute | solution.py:180
  15.0 4.7 %collective-permute-done.2.end0 = f32[2,256,256]{2,1,0:T(8,128)S(1)} collective-permute-done((f32[2,256,256]{2,1,0:T(8,128)}, f32[2,256,256]{2,1,0:T(8,128)S(1)}, u32[]{:S(2)}, u32[]{:S(2)}) %collective-permute-start.2) | collective-permute-done | bytes 524320 | tf_op jit(solution)/shard_map/ppermute | solution.py:180
  20.4 1.3 collective-permute-start.5
  21.7 5.4 %collective-permute-start.3 = (f32[2,256,256]{2,1,0:T(8,128)}, f32[2,256,256]{2,1,0:T(8,128)}, u32[]{:S(2)}, u32[]{:S(2)}) collective-permute-start(f32[2,256,256]{2,1,0:T(8,128)} %own.2), channel_id=1, source_target_pairs={{0,1},{3,2},{4,5},{7,6},{8,9},{11,10},{12,13},{15,14},{16,17},{19,... | collective-permute-start | bytes 1572872 | tf_op jit(solution)/shard_map/ppermute | solution.py:180
  27.1 7.7 %collective-permute-done.5.end1 = f32[2,256,256]{2,1,0:T(8,128)S(1)} collective-permute-done((f32[2,256,256]{2,1,0:T(8,128)S(1)}, f32[2,256,256]{2,1,0:T(8,128)S(1)}, u32[]{:S(2)}, u32[]{:S(2)}) %collective-permute-start.5) | collective-permute-done | bytes 524320 | tf_op jit(solution)/shard_map/ppermute | solution.py:180
  34.8 1.4 %collective-permute-start.7 = (f32[2,256,256]{2,1,0:T(8,128)}, f32[2,256,256]{2,1,0:T(8,128)}, u32[]{:S(2)}, u32[]{:S(2)}) collective-permute-start(f32[2,256,256]{2,1,0:T(8,128)} %own.2), channel_id=1, source_target_pairs={{1,2},{2,1},{5,6},{6,5},{9,10},{10,9},{13,14},{14,13},{17,18},{18,... | collective-permute-start | bytes 1572872 | tf_op jit(solution)/shard_map/ppermute | solution.py:180
  36.2 1.3 collective-permute-start.11
  37.5 1.5 %collective-permute-start.9 = (f32[2,256,256]{2,1,0:T(8,128)}, f32[2,256,256]{2,1,0:T(8,128)}, u32[]{:S(2)}, u32[]{:S(2)}) collective-permute-start(f32[2,256,256]{2,1,0:T(8,128)} %collective-permute-done.3.inner0), channel_id=1, source_target_pairs={{1,2},{2,1},{5,6},{6,5},{9,10},{10,9},{13,14},{14,13},{17,18},{18,... | collective-permute-start | bytes 1572872 | tf_op jit(solution)/shard_map/ppermute | solution.py:180
  39.0 1.3 collective-permute-start.6
  40.3 1.3 collective-permute-start.8
  41.6 1.6 %copy-done = f32[2,256,1024]{2,1,0:T(8,128)S(1)} copy-done((f32[2,256,1024]{2,1,0:T(8,128)S(1)}, f32[2,256,1024]{2,1,0:T(8,128)}, u32[]{:S(2)}) %copy-start) | copy-done | bytes 2097176
  43.2 1.0 copy-done.2
  44.2 1.0 near.3
  45.3 7.8 %collective-permute-done.11.end2 = f32[2,256,256]{2,1,0:T(8,128)} collective-permute-done((f32[2,256,256]{2,1,0:T(8,128)S(1)}, f32[2,256,256]{2,1,0:T(8,128)}, u32[]{:S(2)}, u32[]{:S(2)}) %collective-permute-start.11) | collective-permute-done | bytes 524320 | tf_op jit(solution)/shard_map/ppermute | solution.py:180
  53.1 2.0 %last.3 = (f32[2,256,256]{2,1,0:T(8,128)S(1)}, f32[2,256,256]{2,1,0:T(8,128)S(1)}) custom-call(f32[2,256,256]{2,1,0:T(8,128)S(1)} %get-tuple-element.32.part, bf16[2,256,256]{2,1,0:T(8,128)(2,1)S(1)} %get-tuple-element.33.far_high, bf16[2,256,256]{2,1,0:T(8,128)(2,1)S(1)} %get-tuple-element.34.far_low, f32[2,256,256]{2,1,0:T(8,128)S(1)} %collective-permute-done.4.across1, ...), custom_call_target="tpu_custom_call" | custom-call | flops 402653184 | bytes 4194304 | tf_op jit(solution)/shard_map/last/pallas_call | solution.py:48
  56.6 10.2 %all-to-all-start.1 = ((f32[8,64,256]{2,1,0:T(8,128)}), f32[8,64,256]{2,1,0:T(8,128)S(1)}, u32[]{:S(2)}, u32[]{:S(2)}) async-start(f32[8,64,256]{2,1,0:T(8,128)} %bitcast.5), calls=%async_computation.1 | async-start | bytes 1048576 | tf_op jit(solution)/shard_map/all_to_all | solution.py:201
  66.8 1.3 collective-permute-start.10
  68.1 13.0 %collective-permute-done.8.end1 = f32[2,256,256]{2,1,0:T(8,128)} collective-permute-done((f32[2,256,256]{2,1,0:T(8,128)}, f32[2,256,256]{2,1,0:T(8,128)}, u32[]{:S(2)}, u32[]{:S(2)}) %collective-permute-start.8) | collective-permute-done | bytes 524320 | tf_op jit(solution)/shard_map/ppermute | solution.py:180
  81.1 1.0 copy-done.7
  82.2 2.5 %near.2 = (f32[2,256,256]{2,1,0:T(8,128)S(1)}, bf16[2,256,256]{2,1,0:T(8,128)(2,1)S(1)}, bf16[2,256,256]{2,1,0:T(8,128)(2,1)S(1)}) custom-call(s32[1]{0:T(128)} %bitcast.place, f32[2,256,1024]{2,1,0:T(8,128)S(1)} %copy-done.1, f32[2,256,256]{2,1,0:T(8,128)S(1)} %copy-done.7, f32[2,256,256]{2,1,0:T(8,128)} %collective-permute-done.3.inner0, ...), custom_call_target="tpu_custom_call" | custom-call | flops 24159191040 | bytes 4194304 | tf_op jit(solution)/shard_map/near/pallas_call | solution.py:48
  86.2 1.2 all-to-all-done.1.pieces
  88.3 3.5 %all-to-all-start.2 = ((f32[4,2,64,256]{3,2,1,0:T(8,128)}), f32[4,2,64,256]{3,2,1,0:T(8,128)S(1)}, u32[]{:S(2)}, u32[]{:S(2)}) async-start(f32[4,2,64,256]{3,2,1,0:T(8,128)} %spread.1), calls=%async_computation.2 | async-start | bytes 1048576 | tf_op jit(solution)/shard_map/all_to_all | solution.py:242
  91.8 4.3 %collective-permute-done.10.end2 = f32[2,256,256]{2,1,0:T(8,128)} collective-permute-done((f32[2,256,256]{2,1,0:T(8,128)}, f32[2,256,256]{2,1,0:T(8,128)}, u32[]{:S(2)}, u32[]{:S(2)}) %collective-permute-start.10) | collective-permute-done | bytes 524320 | tf_op jit(solution)/shard_map/ppermute | solution.py:180
  96.1 2.9 %last.2 = (f32[2,256,256]{2,1,0:T(8,128)S(1)}, f32[2,256,256]{2,1,0:T(8,128)}) custom-call(f32[2,256,256]{2,1,0:T(8,128)S(1)} %copy-done.9, bf16[2,256,256]{2,1,0:T(8,128)(2,1)S(1)} %get-tuple-element.27.far_high, bf16[2,256,256]{2,1,0:T(8,128)(2,1)S(1)} %copy-done.11, f32[2,256,256]{2,1,0:T(8,128)} %collective-permute-done.9.across1, ...), custom_call_target="tpu_custom_call" | custom-call | flops 16106127360 | bytes 4194304 | tf_op jit(solution)/shard_map/last/pallas_call | solution.py:48
  99.0 3.0 %all-to-all-done.2.gathered = f32[4,2,64,256]{3,2,1,0:T(8,128)S(1)} async-done(((f32[4,2,64,256]{3,2,1,0:T(8,128)}), f32[4,2,64,256]{3,2,1,0:T(8,128)S(1)}, u32[]{:S(2)}, u32[]{:S(2)}) %all-to-all-start.2) | async-done | bytes 524320 | tf_op jit(solution)/shard_map/all_to_all | solution.py:242
  102.0 5.8 %all-to-all-start = ((f32[8,64,256]{2,1,0:T(8,128)}), f32[8,64,256]{2,1,0:T(8,128)S(1)}, u32[]{:S(2)}, u32[]{:S(2)}) async-start(f32[8,64,256]{2,1,0:T(8,128)} %bitcast.1), calls=%async_computation | async-start | bytes 1048576 | tf_op jit(solution)/shard_map/all_to_all | solution.py:201
  107.8 2.5 %invert.1.inverse = f32[256,256]{1,0:T(8,128)S(1)} custom-call(f32[4,2,64,256]{3,2,1,0:T(8,128)S(1)} %all-to-all-done.2.gathered), custom_call_target="tpu_custom_call" | custom-call | flops 1006632960 | bytes 4194304 | tf_op jit(solution)/shard_map/invert/pallas_call | solution.py:48
  110.3 9.6 %all-to-all-done.pieces = f32[8,64,256]{2,1,0:T(8,128)S(1)} async-done(((f32[8,64,256]{2,1,0:T(8,128)}), f32[8,64,256]{2,1,0:T(8,128)S(1)}, u32[]{:S(2)}, u32[]{:S(2)}) %all-to-all-start) | async-done | bytes 524320 | tf_op jit(solution)/shard_map/all_to_all | solution.py:201
  120.6 14.8 %all_to_all.20 = f32[8,64,256]{2,1,0:T(8,128)S(1)} all-to-all(f32[8,64,256]{2,1,0:T(8,128)S(1)} %coeffs.1), channel_id=1, replica_groups={{0,1,2,3,16,17,18,19},{4,5,6,7,20,21,22,23},{8,9,10,11,24,25,26,27},{12..., dimensions={0} | all-to-all | bytes 1048576 | tf_op jit(solution)/shard_map/all_to_all | solution.py:201
  135.4 1.2 final.1
  (31 shorter events, 6.0 us)
Async XLA Ops:
  0.0 15.0 %collective-permute-start = (f32[2,256,256]{2,1,0:T(8,128)}, f32[2,256,256]{2,1,0:T(8,128)S(1)}, u32[]{:S(2)}, u32[]{:S(2)}) collective-permute-start(f32[2,256,256]{2,1,0:T(8,128)} %own.3), channel_id=1, source_target_pairs={{0,1},{3,2},{4,5},{7,6},{8,9},{11,10},{12,13},{15,14},{16,17},{19,... | collective-permute-start | bytes 1572872 | tf_op jit(solution)/shard_map/ppermute | solution.py:180
  3.5 11.5 %collective-permute-start.1 = (f32[2,256,256]{2,1,0:T(8,128)}, f32[2,256,256]{2,1,0:T(8,128)S(1)}, u32[]{:S(2)}, u32[]{:S(2)}) collective-permute-start(f32[2,256,256]{2,1,0:T(8,128)} %own.3), channel_id=1, source_target_pairs={{1,2},{2,1},{5,6},{6,5},{9,10},{10,9},{13,14},{14,13},{17,18},{18,... | collective-permute-start | bytes 1572872 | tf_op jit(solution)/shard_map/ppermute | solution.py:180
  4.2 15.5 %collective-permute-start.2 = (f32[2,256,256]{2,1,0:T(8,128)}, f32[2,256,256]{2,1,0:T(8,128)S(1)}, u32[]{:S(2)}, u32[]{:S(2)}) collective-permute-start(f32[2,256,256]{2,1,0:T(8,128)} %own.3), channel_id=1, source_target_pairs={{1,0},{2,3},{5,4},{6,7},{9,8},{10,11},{13,12},{14,15},{17,16},{18,... | collective-permute-start | bytes 1572872 | tf_op jit(solution)/shard_map/ppermute | solution.py:180
  19.7 7.4 %collective-permute-start.4 = (f32[2,256,256]{2,1,0:T(8,128)S(1)}, f32[2,256,256]{2,1,0:T(8,128)S(1)}, u32[]{:S(2)}, u32[]{:S(2)}) collective-permute-start(f32[2,256,256]{2,1,0:T(8,128)S(1)} %collective-permute-done.inner0), channel_id=1, source_target_pairs={{1,2},{2,1},{5,6},{6,5},{9,10},{10,9},{13,14},{14,13},{17,18},{18,... | collective-permute-start | bytes 1572872 | tf_op jit(solution)/shard_map/ppermute | solution.py:180
  20.4 14.4 %collective-permute-start.5 = (f32[2,256,256]{2,1,0:T(8,128)S(1)}, f32[2,256,256]{2,1,0:T(8,128)S(1)}, u32[]{:S(2)}, u32[]{:S(2)}) collective-permute-start(f32[2,256,256]{2,1,0:T(8,128)S(1)} %collective-permute-done.1.across0), channel_id=1, source_target_pairs={{1,0},{2,3},{5,4},{6,7},{9,8},{10,11},{13,12},{14,15},{17,16},{18,... | collective-permute-start | bytes 1572872 | tf_op jit(solution)/shard_map/ppermute | solution.py:180
  21.7 15.8 %collective-permute-start.3 = (f32[2,256,256]{2,1,0:T(8,128)}, f32[2,256,256]{2,1,0:T(8,128)}, u32[]{:S(2)}, u32[]{:S(2)}) collective-permute-start(f32[2,256,256]{2,1,0:T(8,128)} %own.2), channel_id=1, source_target_pairs={{0,1},{3,2},{4,5},{7,6},{8,9},{11,10},{12,13},{15,14},{16,17},{19,... | collective-permute-start | bytes 1572872 | tf_op jit(solution)/shard_map/ppermute | solution.py:180
  34.8 5.5 %collective-permute-start.7 = (f32[2,256,256]{2,1,0:T(8,128)}, f32[2,256,256]{2,1,0:T(8,128)}, u32[]{:S(2)}, u32[]{:S(2)}) collective-permute-start(f32[2,256,256]{2,1,0:T(8,128)} %own.2), channel_id=1, source_target_pairs={{1,2},{2,1},{5,6},{6,5},{9,10},{10,9},{13,14},{14,13},{17,18},{18,... | collective-permute-start | bytes 1572872 | tf_op jit(solution)/shard_map/ppermute | solution.py:180
  36.2 16.8 %collective-permute-start.11 = (f32[2,256,256]{2,1,0:T(8,128)S(1)}, f32[2,256,256]{2,1,0:T(8,128)}, u32[]{:S(2)}, u32[]{:S(2)}) collective-permute-start(f32[2,256,256]{2,1,0:T(8,128)S(1)} %collective-permute-done.4.across1), channel_id=1, source_target_pairs={{1,0},{2,3},{5,4},{6,7},{9,8},{10,11},{13,12},{14,15},{17,16},{18,... | collective-permute-start | bytes 1572872 | tf_op jit(solution)/shard_map/ppermute | solution.py:180
  37.5 29.3 %collective-permute-start.9 = (f32[2,256,256]{2,1,0:T(8,128)}, f32[2,256,256]{2,1,0:T(8,128)}, u32[]{:S(2)}, u32[]{:S(2)}) collective-permute-start(f32[2,256,256]{2,1,0:T(8,128)} %collective-permute-done.3.inner0), channel_id=1, source_target_pairs={{1,2},{2,1},{5,6},{6,5},{9,10},{10,9},{13,14},{14,13},{17,18},{18,... | collective-permute-start | bytes 1572872 | tf_op jit(solution)/shard_map/ppermute | solution.py:180
  39.0 29.1 %collective-permute-start.6 = (f32[2,256,256]{2,1,0:T(8,128)}, f32[2,256,256]{2,1,0:T(8,128)}, u32[]{:S(2)}, u32[]{:S(2)}) collective-permute-start(f32[2,256,256]{2,1,0:T(8,128)} %own.2), channel_id=1, source_target_pairs={{1,0},{2,3},{5,4},{6,7},{9,8},{10,11},{13,12},{14,15},{17,16},{18,... | collective-permute-start | bytes 1572872 | tf_op jit(solution)/shard_map/ppermute | solution.py:180
  40.3 40.9 %collective-permute-start.8 = (f32[2,256,256]{2,1,0:T(8,128)}, f32[2,256,256]{2,1,0:T(8,128)}, u32[]{:S(2)}, u32[]{:S(2)}) collective-permute-start(f32[2,256,256]{2,1,0:T(8,128)} %collective-permute-done.7.across0), channel_id=1, source_target_pairs={{1,0},{2,3},{5,4},{6,7},{9,8},{10,11},{13,12},{14,15},{17,16},{18,... | collective-permute-start | bytes 1572872 | tf_op jit(solution)/shard_map/ppermute | solution.py:180
  41.6 1.6 %copy-start = (f32[2,256,1024]{2,1,0:T(8,128)S(1)}, f32[2,256,1024]{2,1,0:T(8,128)}, u32[]{:S(2)}) copy-start(f32[2,256,1024]{2,1,0:T(8,128)} %inverse.3) | copy-start | bytes 6291460
  43.2 1.0 copy-start.2
  44.2 8.9 %copy-start.3 = (f32[2,256,256]{2,1,0:T(8,128)S(1)}, f32[2,256,256]{2,1,0:T(8,128)}, u32[]{:S(2)}) copy-start(f32[2,256,256]{2,1,0:T(8,128)} %right.3) | copy-start | bytes 1572868
  45.2 35.9 %copy-start.1 = (f32[2,256,1024]{2,1,0:T(8,128)S(1)}, f32[2,256,1024]{2,1,0:T(8,128)}, u32[]{:S(2)}) copy-start(f32[2,256,1024]{2,1,0:T(8,128)} %inverse.3) | copy-start | bytes 6291460
  55.0 0.8 copy-start.5
  55.8 0.8 copy-start.4
  56.6 30.8 %all-to-all-start.1 = ((f32[8,64,256]{2,1,0:T(8,128)}), f32[8,64,256]{2,1,0:T(8,128)S(1)}, u32[]{:S(2)}, u32[]{:S(2)}) async-start(f32[8,64,256]{2,1,0:T(8,128)} %bitcast.5), calls=%async_computation.1 | async-start | bytes 1048576 | tf_op jit(solution)/shard_map/all_to_all | solution.py:201
  66.8 29.3 %collective-permute-start.10 = (f32[2,256,256]{2,1,0:T(8,128)}, f32[2,256,256]{2,1,0:T(8,128)}, u32[]{:S(2)}, u32[]{:S(2)}) collective-permute-start(f32[2,256,256]{2,1,0:T(8,128)} %collective-permute-done.9.across1), channel_id=1, source_target_pairs={{1,0},{2,3},{5,4},{6,7},{9,8},{10,11},{13,12},{14,15},{17,16},{18,... | collective-permute-start | bytes 1572872 | tf_op jit(solution)/shard_map/ppermute | solution.py:180
  81.1 1.0 copy-start.7
  84.7 0.8 copy-start.8
  85.5 0.7 copy-start.10
  87.5 8.6 %copy-start.9 = (f32[2,256,256]{2,1,0:T(8,128)S(1)}, f32[2,256,256]{2,1,0:T(8,128)}, u32[]{:S(2)}) copy-start(f32[2,256,256]{2,1,0:T(8,128)} %copy-done.8) | copy-start | bytes 1572868
  87.5 8.6 %copy-start.11 = (bf16[2,256,256]{2,1,0:T(8,128)(2,1)S(1)}, bf16[2,256,256]{2,1,0:T(8,128)(2,1)}, u32[]{:S(2)}) copy-start(bf16[2,256,256]{2,1,0:T(8,128)(2,1)} %copy-done.10) | copy-start | bytes 786436
  88.3 13.7 %all-to-all-start.2 = ((f32[4,2,64,256]{3,2,1,0:T(8,128)}), f32[4,2,64,256]{3,2,1,0:T(8,128)S(1)}, u32[]{:S(2)}, u32[]{:S(2)}) async-start(f32[4,2,64,256]{3,2,1,0:T(8,128)} %spread.1), calls=%async_computation.2 | async-start | bytes 1048576 | tf_op jit(solution)/shard_map/all_to_all | solution.py:242
  102.0 17.9 %all-to-all-start = ((f32[8,64,256]{2,1,0:T(8,128)}), f32[8,64,256]{2,1,0:T(8,128)S(1)}, u32[]{:S(2)}, u32[]{:S(2)}) async-start(f32[8,64,256]{2,1,0:T(8,128)} %bitcast.1), calls=%async_computation | async-start | bytes 1048576 | tf_op jit(solution)/shard_map/all_to_all | solution.py:201
  110.3 25.1 %copy-start.6 = (f32[2,256,256]{2,1,0:T(8,128)S(1)}, f32[2,256,256]{2,1,0:T(8,128)}, u32[]{:S(2)}) copy-start(f32[2,256,256]{2,1,0:T(8,128)} %copy-done.5) | copy-start | bytes 1572868
